TPU v7x, 256 devices: a whole 4x4x8 slice. The times are simulated.
256 devices in a mesh: row: 32 (over z_lo, x, core), col: 8 (over z_hi, y).
Axes of the slice: x: 4, y: 4, z: 8 (z_hi: 2, z_lo: 4; z = z_hi * 4 + z_lo), core: 2. Of those that a mesh axis runs over, the one named last changes fastest.
Arguments:
- sequence_stack: bfloat16 [64, 1024, 256], P(None, 'row'), may hold values from -6 to 6
- feature_multiplier: float32 [256], replicated, may hold values from 0.1 to 1.9
- first_factor_map: bfloat16 [256, 32], replicated, may hold values from -0.375 to 0.375
- second_factor_map: bfloat16 [256, 32], replicated, may hold values from -0.375 to 0.375
- emitted_map: bfloat16 [1024, 128], replicated, may hold values from -1.5 to 1.5
- emitted_offset: float32 [128], replicated, may hold values from -3 to 3
- upstream_adjoint: bfloat16 [1024, 1024, 128], P('row', 'col'), may hold values from -0.59765625 to 0.59765625
Outputs:
- pair_update: bfloat16 [1024, 1024, 128], P('row', 'col')
- sequence_stack_adjoint: float32 [64, 1024, 256], P(None, 'row')
- factor_maps_adjoint: float32 [2, 256, 32], replicated
- emitted_map_adjoint: float32 [1024, 128], replicated
- emitted_offset_adjoint: float32 [128], replicated
All inputs are finite; a program needn't handle non-finite values.
Results may differ from a plain program's by a relative error of at most 0.0072.
Values may be sent and summed in bfloat16 or wider, within the bound.
A program may use at most 64 MiB of HBM per device.

v0:
```python
import math

import jax
import jax.numpy as jnp
from jax import lax
from jax.sharding import PartitionSpec as P


def rescale_features(sequence_stack, feature_multiplier):
    quantity_elements = sequence_stack.astype(jnp.float32)
    average = jnp.mean(quantity_elements, -1, keepdims=True)
    centered = quantity_elements - average
    variance = jnp.mean(centered * centered, -1, keepdims=True)
    reciprocal_spread = lax.rsqrt(variance + 1e-05)
    spread_estimate = centered * reciprocal_spread
    whitened_features = (spread_estimate * feature_multiplier).astype(jnp.bfloat16)
    return (spread_estimate, reciprocal_spread, whitened_features)


def project(whitened_features, weight_matrix):
    alignment_rows, residue_count, channel_count = whitened_features.shape
    flattened_rows = jnp.dot(
        whitened_features.reshape(alignment_rows * residue_count, channel_count),
        weight_matrix,
        preferred_element_type=jnp.float32,
    )
    return flattened_rows.reshape(alignment_rows, residue_count, weight_matrix.shape[1]).astype(
        jnp.bfloat16
    )


def pair_block(left_block, right_columns, emitted_map, emitted_offset, cot_blk):
    alignment_rows, local_rows, channel_count = left_block.shape
    column_count = right_columns.shape[1]
    left_flattened = left_block.reshape(alignment_rows, local_rows * channel_count)
    right_flattened = right_columns.reshape(alignment_rows, column_count * channel_count)
    outer_result = jnp.dot(
        left_flattened.T, right_flattened, preferred_element_type=jnp.float32
    ) * (1.0 / alignment_rows)
    outer = outer_result.reshape(local_rows, channel_count, column_count, channel_count).transpose(
        0, 2, 1, 3
    )
    outer = outer.reshape(local_rows * column_count, channel_count * channel_count).astype(
        jnp.bfloat16
    )
    coupling_increment = (
        jnp.dot(outer, emitted_map, preferred_element_type=jnp.float32) + emitted_offset
    ).astype(jnp.bfloat16)
    cot_rows = cot_blk.reshape(local_rows * column_count, cot_blk.shape[2])
    weight_gradient = jnp.dot(outer.T, cot_rows, preferred_element_type=jnp.float32)
    bias_gradient = jnp.sum(cot_rows.astype(jnp.float32), 0)
    d_outer = jnp.dot(cot_rows, emitted_map.T, preferred_element_type=jnp.float32).astype(
        jnp.bfloat16
    )
    ordered_layout = d_outer.reshape(
        local_rows, column_count, channel_count, channel_count
    ).transpose(0, 2, 1, 3)
    ordered_layout = ordered_layout.reshape(
        local_rows * channel_count, column_count * channel_count
    )
    first_factor_adjoint = jnp.dot(
        right_flattened, ordered_layout.T, preferred_element_type=jnp.float32
    ) * (1.0 / alignment_rows)
    second_factor_adjoint = jnp.dot(
        left_flattened, ordered_layout, preferred_element_type=jnp.float32
    ) * (1.0 / alignment_rows)
    return (
        coupling_increment.reshape(local_rows, column_count, emitted_map.shape[1]),
        weight_gradient,
        bias_gradient,
        first_factor_adjoint.reshape(alignment_rows, local_rows, channel_count),
        second_factor_adjoint.reshape(alignment_rows, column_count, channel_count),
    )


def sweep_pairs(
    left_side, right_columns, emitted_map, emitted_offset, upstream_adjoint, block_rows
):
    alignment_rows, residue_count, channel_count = left_side.shape
    column_count = right_columns.shape[1]
    blocks = residue_count // block_rows
    initial_totals = (
        jnp.zeros(emitted_map.shape, jnp.float32),
        jnp.zeros((emitted_map.shape[1],), jnp.float32),
        jnp.zeros((alignment_rows, column_count, channel_count), jnp.float32),
    )

    def advance(totals, block_index):
        offset = block_index * block_rows
        left_block = lax.dynamic_slice_in_dim(left_side, offset, block_rows, 1)
        cot_blk = lax.dynamic_slice_in_dim(upstream_adjoint, offset, block_rows, 0)
        (
            coupling_increment,
            weight_gradient,
            bias_gradient,
            first_factor_adjoint,
            second_factor_adjoint,
        ) = pair_block(left_block, right_columns, emitted_map, emitted_offset, cot_blk)
        return (
            (
                totals[0] + weight_gradient,
                totals[1] + bias_gradient,
                totals[2] + second_factor_adjoint,
            ),
            (coupling_increment, first_factor_adjoint),
        )

    totals, (updates, left_sides) = lax.scan(
        advance, initial_totals, jnp.arange(blocks, dtype=jnp.int32)
    )
    coupling_increment = updates.reshape(residue_count, column_count, emitted_map.shape[1])
    first_factor_adjoint = left_sides.transpose(1, 0, 2, 3).reshape(
        alignment_rows, residue_count, channel_count
    )
    return (coupling_increment, totals[0], totals[1], first_factor_adjoint, totals[2])


def closing_iteration(
    whitened_features,
    spread_estimate,
    reciprocal_spread,
    feature_multiplier,
    first_factor_map,
    second_factor_map,
    first_factor_adjoint,
    second_factor_adjoint,
):
    alignment_rows, residue_count, channel_count = whitened_features.shape
    left_gradient16 = first_factor_adjoint.astype(jnp.bfloat16).reshape(
        alignment_rows * residue_count, -1
    )
    right_gradient16 = second_factor_adjoint.astype(jnp.bfloat16).reshape(
        alignment_rows * residue_count, -1
    )
    normalized_flattened = whitened_features.reshape(alignment_rows * residue_count, channel_count)
    normalized_gradient = jnp.dot(
        left_gradient16, first_factor_map.T, preferred_element_type=jnp.float32
    )
    normalized_gradient = normalized_gradient + jnp.dot(
        right_gradient16, second_factor_map.T, preferred_element_type=jnp.float32
    )
    stretched_features = (
        normalized_gradient.reshape(alignment_rows, residue_count, channel_count)
        * feature_multiplier
    )
    sequence_stack_adjoint = reciprocal_spread * (
        stretched_features
        - jnp.mean(stretched_features, -1, keepdims=True)
        - spread_estimate * jnp.mean(stretched_features * spread_estimate, -1, keepdims=True)
    )
    factor_maps_adjoint = jnp.stack(
        [
            jnp.dot(normalized_flattened.T, left_gradient16, preferred_element_type=jnp.float32),
            jnp.dot(normalized_flattened.T, right_gradient16, preferred_element_type=jnp.float32),
        ]
    )
    return (sequence_stack_adjoint, factor_maps_adjoint)


def per_device(
    sequence_stack,
    feature_multiplier,
    first_factor_map,
    second_factor_map,
    emitted_map,
    emitted_offset,
    upstream_adjoint,
):
    sequences_per_tile = sequence_stack.shape[1]
    column_count = upstream_adjoint.shape[1]
    owned = column_count // sequences_per_tile
    col_place = lax.axis_index("col")
    spread_estimate, reciprocal_spread, whitened_features = rescale_features(
        sequence_stack, feature_multiplier
    )
    left_side = project(whitened_features, first_factor_map)
    right = project(whitened_features, second_factor_map)
    gathered = lax.all_gather(right, "row", axis=1, tiled=True)
    right_columns = lax.dynamic_slice_in_dim(gathered, col_place * column_count, column_count, 1)
    block_rows = math.gcd(sequences_per_tile, max(1, 1024 // column_count))
    coupling_increment, grad_w_part, grad_b_part, left_part, right_part = sweep_pairs(
        left_side, right_columns, emitted_map, emitted_offset, upstream_adjoint, block_rows
    )
    summed = lax.psum(right_part, "row")
    member = lax.axis_index("row") - owned * col_place
    inside = ((member >= 0) & (member < owned)).astype(jnp.float32)
    picked = lax.dynamic_slice_in_dim(
        summed, jnp.clip(member, 0, owned - 1) * sequences_per_tile, sequences_per_tile, 1
    )
    right_mine = picked * inside
    first_factor_adjoint, second_factor_adjoint = lax.psum((left_part, right_mine), "col")
    sequence_stack_adjoint, factor_maps_share = closing_iteration(
        whitened_features,
        spread_estimate,
        reciprocal_spread,
        feature_multiplier,
        first_factor_map,
        second_factor_map,
        first_factor_adjoint,
        second_factor_adjoint,
    )
    factor_maps_adjoint = lax.psum(factor_maps_share, "row")
    emitted_map_adjoint, emitted_offset_adjoint = lax.psum(
        (grad_w_part, grad_b_part), ("row", "col")
    )
    return (
        coupling_increment,
        sequence_stack_adjoint,
        factor_maps_adjoint,
        emitted_map_adjoint,
        emitted_offset_adjoint,
    )


def solution(mesh):
    return jax.shard_map(
        per_device,
        mesh=mesh,
        in_specs=(P(None, "row", None), P(), P(), P(), P(), P(), P("row", "col", None)),
        out_specs=(P("row", "col", None), P(None, "row", None), P(), P(), P()),
        check_vma=False,
    )
```

profile of v0, /device:TPU:1, one launch (start us, length us, event | category | flops | bytes accessed | tf_op | source)
XLA Modules:
  0.0 1174.4 jit_solution(5008225055075394224)
XLA Ops:
  15.0 101.7 %all-gather.2.cloned.1.call-done = bf16[64,1024,32]{2,1,0:T(8,128)(2,1)} async-done(((bf16[64,32,32]{2,1,0:T(8,128)(2,1)}), bf16[64,1024,32]{2,1,0:T(8,128)(2,1)}) %all-gather.2.cloned.1.call-update) | async-done | bytes 4194320 | tf_op jit(solution)/shard_map/all_gather | solution.py:178
  118.4 2.2 copy.22
  121.2 256.2 %while.19 = (s32[]{:T(128)}, f32[1024,128]{1,0:T(8,128)}, f32[128]{0:T(128)}, f32[64,128,32]{0,2,1:T(8,128)}, bf16[4,8,128,128]{3,2,1,0:T(8,128)(2,1)}, /*index=...) while((s32[]{:T(128)}, f32[1024,128]{1,0:T(8,128)}, ...), condition=%wide.region_4.5_spmd.clone, body=%wide.region_2.4_spmd.clone.sunk | while | flops 1212694656 | bytes 50079568 | solution.py:108
  126.5 2.6 copy.58
  129.1 2.2 copy.59
  131.3 5.9 copy.60
  137.2 10.7 reshape.108
  150.2 3.2 copy.61
  153.4 3.4 select_add_fusion.2
  158.9 9.4 convert_element_type.106
  168.3 8.1 copy.57
  176.4 3.1 fusion.81
  181.1 2.4 fusion.83
  190.0 2.6 copy.58
  192.6 2.2 copy.59
  194.8 5.9 copy.60
  200.7 10.7 reshape.108
  213.7 3.2 copy.61
  216.9 4.0 select_add_fusion.2
  223.0 9.4 convert_element_type.106
  232.4 8.1 copy.57
  240.5 3.2 fusion.81
  245.3 2.4 fusion.83
  254.2 2.6 copy.58
  256.8 2.2 copy.59
  259.0 5.9 copy.60
  264.9 10.7 reshape.108
  277.9 3.2 copy.61
  281.1 4.0 select_add_fusion.2
  287.3 9.4 convert_element_type.106
  296.6 8.1 copy.57
  304.8 3.2 fusion.81
  309.5 2.4 fusion.83
  318.5 2.6 copy.58
  323.2 5.9 copy.60
  329.2 10.7 reshape.108
  342.2 3.2 copy.61
  345.3 4.0 select_add_fusion.2
  351.5 9.4 convert_element_type.106
  360.8 8.1 copy.57
  369.0 3.2 fusion.81
  373.7 2.4 fusion.83
  378.0 78.0 %psum.47 = f32[128]{0:T(128)} all-reduce(f32[128]{0:T(128)S(1)} %copy-done.10), channel_id=1, replica_groups=mesh['row'=32,'col'=8] {'row','col'}, use_global_device_ids=true, to_apply=%region_12.13 | all-reduce | flops 128 | bytes 1024 | tf_op jit(solution)/shard_map/psum | solution.py:203
  456.1 203.6 %all-reduce.6.cloned.1.call-done = f32[64,128,32]{0,2,1:T(8,128)} async-done(((f32[64,128,32]{0,2,1:T(8,128)}), f32[64,128,32]{0,2,1:T(8,128)}) %all-reduce.6.cloned.1.call-update) | async-done | bytes 1048592 | tf_op jit(solution)/shard_map/psum | solution.py:184
  660.8 89.3 %all-reduce.11 = (bf16[64,32,32]{0,2,1:T(8,128)(2,1)S(1)}, bf16[64,32,32]{0,2,1:T(8,128)(2,1)S(1)}) all-reduce(f32[64,32,32]{0,2,1:T(8,128)S(1)} %bitcast.135, f32[64,32,32]{0,2,1:T(8,128)S(1)} %dynamic-slice_multiply_fusion), channel_id=1, replica_groups=mesh['row'=32,'col'=8] {'col'}, use_global_device_ids=true, to_apply=%region_5.6 | all-reduce | flops 131072 | bytes 786432 | tf_op jit(solution)/shard_map/psum | solution.py:191
  763.0 2.2 fusion.26
  765.3 153.6 %all-reduce.10.cloned.1.call-done = f32[1024,128]{1,0:T(8,128)} async-done(((f32[1024,128]{1,0:T(8,128)}), f32[1024,128]{1,0:T(8,128)}) %all-reduce.10.cloned.1.call-update) | async-done | bytes 524304 | tf_op jit(solution)/shard_map/psum | solution.py:203
  918.9 245.7 %all-reduce.8.cloned.1.call-done = f32[2,256,32]{1,2,0:T(8,128)} async-done(((f32[2,256,32]{1,2,0:T(8,128)}), f32[2,256,32]{1,2,0:T(8,128)}) %all-reduce.8.cloned.1.call-update) | async-done | bytes 65552 | tf_op jit(solution)/shard_map/psum | solution.py:202
  (135 shorter events, 77.3 us)
Async XLA Ops:
  7.2 3.6 copy-start
  7.2 3.6 copy-start.1
  7.2 3.6 copy-start.11
  7.2 109.5 %all-gather.2.cloned.1.call-start = ((), (), s32[]{:S(2)}) async-start(), calls=%async_computation | async-start | bytes 17301504 | tf_op jit(solution)/shard_map/all_gather | solution.py:178
  8.9 3.8 copy-start.6
  12.6 647.1 %all-reduce.6.cloned.1.call-start = ((), (), s32[]{:S(2)}) async-start(), calls=%async_computation.1 | async-start | bytes 4194304 | tf_op jit(solution)/shard_map/psum | solution.py:184
  179.5 1.5 copy-start.3
  181.1 3.1 copy-start.5
  181.1 3.1 copy-start.8
  184.2 0.5 copy-start.9
  243.7 1.5 copy-start.3
  245.3 3.1 copy-start.5
  245.3 3.1 copy-start.8
  248.4 0.5 copy-start.9
  307.9 1.5 copy-start.3
  309.5 3.1 copy-start.5
  309.5 3.1 copy-start.8
  312.6 0.5 copy-start.9
  372.2 1.5 copy-start.3
  373.7 3.1 copy-start.5
  373.7 3.1 copy-start.8
  376.8 0.5 copy-start.9
  377.3 0.7 copy-start.10
  377.3 283.4 %copy-start.4 = (f32[4,64,8,32]{1,3,2,0:T(8,128)S(1)}, f32[4,64,8,32]{1,3,2,0:T(8,128)}, u32[]{:S(2)}) copy-start(f32[4,64,8,32]{1,3,2,0:T(8,128)} %get-tuple-element.72) | copy-start | bytes 786436
  377.4 541.5 %all-reduce.10.cloned.1.call-start = ((), (), s32[]{:S(2)}) async-start(), calls=%async_computation.3 | async-start | bytes 1048576 | tf_op jit(solution)/shard_map/psum | solution.py:203
  456.1 708.5 %all-reduce.8.cloned.1.call-start = ((), (), s32[]{:S(2)}) async-start(), calls=%async_computation.2 | async-start | bytes 131072 | tf_op jit(solution)/shard_map/psum | solution.py:202
  660.8 92.4 %copy-start.2 = (bf16[64,32,256]{2,1,0:T(8,128)(2,1)S(1)}, bf16[64,32,256]{2,1,0:T(8,128)(2,1)}, u32[]{:S(2)}) copy-start(bf16[64,32,256]{2,1,0:T(8,128)(2,1)} %param.9) | copy-start | bytes 3145732
  660.8 92.4 %copy-start.12 = (f32[256]{0:T(256)S(1)}, f32[256]{0:T(256)}, u32[]{:S(2)}) copy-start(f32[256]{0:T(256)} %param.10) | copy-start | bytes 3076
  755.3 1.4 copy-start.7
Sparse Core Ops, SparseCore 0:
  12.7 103.9 all-gather.1
  377.5 282.1 all-reduce.5
  666.6 252.1 all-reduce.9
  922.1 242.4 all-reduce.7
where the time goes:
time: 1180 us; the launch traced here: 1170 us
  waiting for transfers between devices  705 us (60%)
  local copies, waits for them, and re-layouts  199 us (17%)
  blocking collectives  167 us (14%)
  matrix products  55.8 us (5%)
  other arithmetic  30.8 us (3%)
  between operations  14.1 us (1%)
    psum x1, waiting for transfers between devices, per_device(): factor_maps_adjoint = lax.psum(factor_maps_share, 'row')  246 us
    psum x1, waiting for transfers between devices, per_device(): summed = lax.psum(right_part, 'row')  204 us
    psum x1, waiting for transfers between devices, per_device(): lax.psum((grad_w_part, grad_b_part), ('row', 'col'))  154 us
    all_gather x1, waiting for transfers between devices, per_device(): gathered = lax.all_gather(right, 'row', axis=1, tiled=True)  102 us
    psum x1, blocking collectives, per_device(): lax.psum((left_part, right_mine), 'col')  89.3 us
    psum x1, blocking collectives, per_device(): lax.psum((grad_w_part, grad_b_part), ('row', 'col'))  78 us
    convert_element_type x8, local copies, waits for them, and re-layouts, pair_block(): outer.reshape(local_rows * column_count, channel_count * channel_count)  70.1 us
    reshape x4, local copies, waits for them, and re-layouts, pair_block(): ordered_layout.reshape(local_rows * channel_count, column_count * channel...  42.6 us
  transfers between devices with their start and end apart: 4, of which 4 were waited for; matrix products, arithmetic and copies ran while one was open for 2% of the time, Pallas kernels for 0%

commit v1 on v0

v1 whole, which is shorter than its diff:
```python
import functools

import jax
import jax.numpy as jnp
from jax import lax
from jax.experimental import pallas as pl
from jax.experimental.pallas import tpu as pltpu
from jax.sharding import PartitionSpec as P

MESH = pl.DeviceIdType.MESH
F32 = jnp.float32
BF16 = jnp.bfloat16
NN = (((1,), (0,)), ((), ()))
NT = (((1,), (1,)), ((), ()))
TN = (((0,), (0,)), ((), ()))


def mm(a, b, dims=NN):
    return lax.dot_general(a, b, dims, preferred_element_type=F32)


def low_lanes(shape):
    return lax.broadcasted_iota(jnp.int32, shape, 1) < 64


def normalise(x):
    average = jnp.mean(x, -1, keepdims=True)
    centered = x - average
    variance = jnp.mean(centered * centered, -1, keepdims=True)
    inverse = lax.rsqrt(variance + 1e-05)
    return centered * inverse, inverse


def project_kernel(x_ref, gain_ref, wt_ref, la_ref, lb_ref, lt_ref, rb_ref, left, right):
    gain = gain_ref[...]
    wt = wt_ref[...]
    low = low_lanes((32, 128))
    low16 = low_lanes((16, 128))

    @pl.loop(0, 8)
    def _(b):
        x = x_ref[pl.ds(b * 4, 4)].astype(F32).reshape(256, 256)
        standard, _ = normalise(x)
        normed = (standard * gain).astype(BF16)
        both = mm(wt, normed, NT).astype(BF16).astype(F32)
        for p in range(2):
            tile = both[:, p * 128 : (p + 1) * 128]
            turned = pltpu.roll(tile, 64, 1)
            row = pl.multiple_of(b * 128 + p * 64, 64)
            scaled, scaled_turned = tile[:32] * (1 / 64), turned[:32] * (1 / 64)
            zero = jnp.zeros_like(scaled)
            la_ref[pl.ds(row, 32)] = jnp.where(low, scaled, zero).astype(BF16)
            lb_ref[pl.ds(row, 32)] = jnp.where(low, zero, scaled_turned).astype(BF16)
            la_ref[pl.ds(row + 32, 32)] = jnp.where(low, scaled_turned, zero).astype(BF16)
            lb_ref[pl.ds(row + 32, 32)] = jnp.where(low, zero, scaled).astype(BF16)
            left[pl.ds(row, 32)] = scaled
            left[pl.ds(row + 32, 32)] = scaled_turned
            j = b * 4 + p * 2
            right[j] = jnp.where(low16, tile[32:48], turned[48:64])
            right[j + 1] = jnp.where(low16, turned[32:48], tile[48:64])

    for b in range(8):
        lt_ref[:, b * 128 : (b + 1) * 128] = left[b * 128 : (b + 1) * 128].T[:64].astype(BF16)
    rb_ref[...] = jnp.swapaxes(right[...], 0, 1).astype(BF16)


def project(x, gain, wt):
    return pl.pallas_call(
        project_kernel,
        out_shape=(
            jax.ShapeDtypeStruct((1024, 128), BF16),
            jax.ShapeDtypeStruct((1024, 128), BF16),
            jax.ShapeDtypeStruct((64, 1024), BF16),
            jax.ShapeDtypeStruct((16, 32, 128), BF16),
        ),
        scratch_shapes=[pltpu.VMEM((1024, 128), F32), pltpu.VMEM((32, 16, 128), F32)],
        compiler_params=pltpu.CompilerParams(vmem_limit_bytes=32 << 20),
        name="project",
    )(x, gain, wt)


def place():
    r = lax.axis_index("row")
    return r, lax.axis_index("col"), r // 8, (r // 2) % 4, r % 2


def serving_half(z, x, z0, zh):
    gap = jnp.abs(z - z0)
    other = jnp.where(gap == 3, 1, jnp.where(gap == 2, (z + x) % 2, 0))
    return (zh + other) % 2


def gather_kernel(rb_ref, out_ref, land, send, recv, swap_send, swap_recv, own_sem):
    r, c, z, x, core = place()
    zh, y = c // 4, c % 4
    sibling = r + 1 - 2 * core
    goal = r // 4
    goal_zh = goal // 4
    k = r % 4
    barrier = pltpu.get_barrier_semaphore()

    for m in range(2):
        owner = 4 * c + core + 2 * m
        half = serving_half(z, x, owner // 8, zh)
        for q in range(4):
            col = half * 4 + q

            @pl.when(jnp.logical_not((owner == r) & (col == c)))
            def _():
                pl.semaphore_signal(barrier, inc=1, device_id=(owner, col), device_id_type=MESH)

    pl.semaphore_signal(barrier, inc=1, device_id=(sibling, c), device_id_type=MESH)

    count = jnp.int32(1)
    for chip in range(16):
        dz, dx = chip // 4, chip % 4
        serves = serving_half(dz, dx, z, goal_zh) == zh
        myself = (goal == c) & (dz == z) & (dx == x)
        count = count + jnp.where(serves & jnp.logical_not(myself), 1, 0)
    pl.semaphore_wait(barrier, count)

    mine = rb_ref.at[pl.ds(y * 4, 4)]
    slot = land.at[pl.ds(y * 4, 4), k]

    def to(dz, dx):
        return pltpu.make_async_remote_copy(
            src_ref=mine,
            dst_ref=slot,
            send_sem=send.at[dz * 4 + dx],
            recv_sem=recv.at[(k // 2) * 4 + y],
            device_id=(dz * 8 + dx * 2 + core, goal),
            device_id_type=MESH,
        )

    def serves_chip(dz, dx):
        serves = serving_half(dz, dx, z, goal_zh) == zh
        return serves, (goal == c) & (dz == z) & (dx == x)

    for step in range(16):
        dz, dx = (z + step // 4) % 4, (x + step % 4) % 4
        serves, myself = serves_chip(dz, dx)

        @pl.when(serves & jnp.logical_not(myself))
        def _():
            to(dz, dx).start()

        if step == 0:

            @pl.when(serves & myself)
            def _():
                own = pltpu.make_async_copy(mine, slot, own_sem)
                own.start()
                own.wait()

    for q in range(4):
        for m in range(2):
            owner = 4 * c + core + 2 * m
            half = serving_half(z, x, owner // 8, zh)
            part = land.at[pl.ds(q * 4, 4), core + 2 * m]

            @pl.when(jnp.logical_not((owner == r) & (half * 4 + q == c)))
            def _():
                pltpu.make_async_remote_copy(
                    src_ref=part,
                    dst_ref=part,
                    send_sem=swap_send.at[m * 4 + q],
                    recv_sem=recv.at[m * 4 + q],
                    device_id=(sibling, c),
                    device_id_type=MESH,
                ).wait_recv()

            pltpu.make_async_remote_copy(
                src_ref=part,
                dst_ref=part,
                send_sem=swap_send.at[m * 4 + q],
                recv_sem=swap_recv.at[m * 4 + q],
                device_id=(sibling, c),
                device_id_type=MESH,
            ).start()

    for step in range(16):
        dz, dx = (z + step // 4) % 4, (x + step % 4) % 4
        serves, myself = serves_chip(dz, dx)

        @pl.when(serves & jnp.logical_not(myself))
        def _():
            to(dz, dx).wait_send()

    for q in range(4):
        for m in range(2):
            part = land.at[pl.ds(q * 4, 4), core + 2 * m]
            there = land.at[pl.ds(q * 4, 4), 1 - core + 2 * m]
            pltpu.make_async_remote_copy(
                src_ref=part,
                dst_ref=there,
                send_sem=swap_send.at[m * 4 + q],
                recv_sem=swap_recv.at[m * 4 + q],
                device_id=(sibling, c),
                device_id_type=MESH,
            ).wait()
    out_ref[...] = land[...]


def gather(rb):
    return pl.pallas_call(
        gather_kernel,
        out_shape=jax.ShapeDtypeStruct((16, 4, 32, 128), BF16),
        in_specs=[pl.BlockSpec(memory_space=pltpu.VMEM)],
        out_specs=pl.BlockSpec(memory_space=pltpu.VMEM),
        scratch_shapes=[
            pltpu.VMEM((16, 4, 32, 128), BF16),
            pltpu.SemaphoreType.DMA((16,)),
            pltpu.SemaphoreType.DMA((8,)),
            pltpu.SemaphoreType.DMA((8,)),
            pltpu.SemaphoreType.DMA((8,)),
            pltpu.SemaphoreType.DMA,
        ],
        compiler_params=pltpu.CompilerParams(
            collective_id=0, has_side_effects=True, vmem_limit_bytes=32 << 20
        ),
        name="gather_right",
    )(rb)


def sweep_kernel(
    la_ref, lb_ref, lt_ref, rt_ref, g_ref, wp_ref, wpt_ref, off_ref,
    pu_ref, sb_ref, gl_ref, bias_ref,
    put, ot, dt, gla, glb, grq, gwq,
):
    @pl.loop(0, 4)
    def _(q):
        right = rt_ref[pl.ds(pl.multiple_of(q * 512, 512), 512)]
        wq = wp_ref[pl.ds(pl.multiple_of(q * 256, 256), 256)]
        wqt = wpt_ref[q]

        @pl.loop(0, 4)
        def _(b):
            rows = pl.ds(pl.multiple_of(b * 256, 256), 256)
            lanes = pl.ds(pl.multiple_of(b * 1024, 1024), 1024)
            g = g_ref[pl.ds(pl.multiple_of(b * 1024, 1024), 1024)]
            for e2, l_ref in enumerate((la_ref, lb_ref)):
                o = mm(l_ref[rows], right, NT).astype(BF16)
                for e1 in range(4):
                    for i in range(8):
                        e = e2 * 4 + e1
                        ot[e * 32 : e * 32 + 32, i * 128 : i * 128 + 128] = o[
                            i * 32 : i * 32 + 32, e1 * 128 : e1 * 128 + 128
                        ]
            d = mm(wq, g, NT).astype(BF16)
            for e in range(8):
                for i in range(8):
                    dt[i * 32 : i * 32 + 32, e * 128 : e * 128 + 128] = d[
                        e * 32 : e * 32 + 32, i * 128 : i * 128 + 128
                    ]
            outer = ot[...]
            update = mm(wqt, outer)
            gw = mm(outer, g)
            left0 = mm(dt[:, :512], right)
            left1 = mm(dt[:, 512:], right)
            gr = mm(lt_ref[b], dt[...])

            @pl.when(q == 0)
            def _():
                put[:, lanes] = update
                gla[rows] = left0
                glb[rows] = left1

            @pl.when(q != 0)
            def _():
                put[:, lanes] += update
                gla[rows] += left0
                glb[rows] += left1

            @pl.when(b == 0)
            def _():
                gwq[...] = gw
                grq[...] = gr

            @pl.when(b != 0)
            def _():
                gwq[...] += gw
                grq[...] += gr

        for core in range(2):
            for z in range(4):
                at = core * 128 + z * 32
                sb_ref[core, q, z, 64:96] = gwq[at : at + 32].astype(BF16)
        for e1 in range(4):
            tile = jnp.concatenate(
                [grq[:, e1 * 128 : e1 * 128 + 128], grq[:, 512 + e1 * 128 : 640 + e1 * 128]], axis=0
            )
            turned = tile.T.astype(BF16)
            for k in range(4):
                at = (e1 % 2) * 32
                sb_ref[k % 2, q, (k // 2) * 2 + e1 // 2, at : at + 32] = turned[k * 32 : k * 32 + 32]

    low = low_lanes((32, 128))
    for m in range(16):
        even, odd = slice(m * 64, m * 64 + 32), slice(m * 64 + 32, m * 64 + 64)
        first = gla[even] + pltpu.roll(glb[even], 64, 1)
        second = glb[odd] + pltpu.roll(gla[odd], 64, 1)
        gl_ref[m * 32 : m * 32 + 32] = (jnp.where(low, first, second) * (1 / 64)).astype(BF16)

    bias_ref[...] = jnp.zeros_like(bias_ref)
    offset = off_ref[...]

    @pl.loop(0, 32)
    def _(i):
        at = pl.ds(pl.multiple_of(i * 128, 128), 128)
        pu_ref[at] = (put[:, at].T + offset).astype(BF16)
        bias_ref[...] += jnp.sum(g_ref[at].astype(F32).reshape(16, 8, 128), 0)


def sweep(la, lb, lt, rt, g, wp, wpt, off):
    return pl.pallas_call(
        sweep_kernel,
        out_shape=(
            jax.ShapeDtypeStruct((4096, 128), BF16),
            jax.ShapeDtypeStruct((2, 4, 4, 96, 128), BF16),
            jax.ShapeDtypeStruct((512, 128), BF16),
            jax.ShapeDtypeStruct((8, 128), F32),
        ),
        scratch_shapes=[
            pltpu.VMEM((128, 4096), F32),
            pltpu.VMEM((256, 1024), BF16),
            pltpu.VMEM((256, 1024), BF16),
            pltpu.VMEM((1024, 128), F32),
            pltpu.VMEM((1024, 128), F32),
            pltpu.VMEM((64, 1024), F32),
            pltpu.VMEM((256, 128), F32),
        ],
        compiler_params=pltpu.CompilerParams(vmem_limit_bytes=48 << 20),
        name="pair_sweep",
    )(la, lb, lt, rt, g, wp, wpt, off)


def copy_to(src, dst, send_sem, recv_sem, device):
    return pltpu.make_async_remote_copy(
        src_ref=src, dst_ref=dst, send_sem=send_sem, recv_sem=recv_sem,
        device_id=device, device_id_type=MESH,
    )


def reduce_kernel(
    sb_ref, gl_ref, fr_ref, fl_ref, w_ref,
    c1, t1, c2, t2, c3, t3, fr, c4, cl, tl, fl,
    s1, r1, s2, r2, s3, r3, s4, r4, s5, r5, s6, r6, s7, r7,
):
    r, c, z, x, core = place()
    sibling = (r + 1 - 2 * core, c)
    k = core + 2 * (z // 2)
    piece = x * 2 + z % 2

    def x_peer(d):
        return z * 8 + ((x + d) % 4) * 2 + core

    def z_peer(d):
        return ((z + d) % 4) * 8 + x * 2 + core

    def source(n):
        kk = r % 4
        return ((kk // 2) * 2 + n % 2) * 8 + (n // 2) * 2 + kk % 2

    barrier = pltpu.get_barrier_semaphore()

    def signal(device):
        pl.semaphore_signal(barrier, inc=1, device_id=device, device_id_type=MESH)

    signal(sibling)
    for d in range(1, 4):
        signal((x_peer(d), c))
        signal((z_peer(d), c))
    for d in range(1, 8):
        signal((r, (c + d) % 8))
    owner = 4 * c + k
    for n in range(8):

        @pl.when(jnp.logical_not((source(n) == r) & (r // 4 == c)))
        def _():
            signal((source(n), r // 4))

    pl.semaphore_wait(barrier, 14 + 8 - jnp.where(owner == r, 1, 0))

    first = []
    for d in (1, 2, 3, 0):
        xx = (x + d) % 4
        cp = copy_to(sb_ref.at[1 - core, xx], c1.at[xx], s1.at[d], r1.at[d], sibling)
        cp.start()
        first.append((d, xx, cp))
    lefts = []
    for d in range(1, 8):
        cc = (c + d) % 8
        cp = copy_to(gl_ref.at[cc], cl.at[d], s5.at[d], r5.at[d], (r, cc))
        cp.start()
        lefts.append(cp)
    second = []
    for d, xx, cp in first:
        cp.wait_recv()
        t1[xx] = (sb_ref[core, xx].astype(F32) + c1[xx].astype(F32)).astype(BF16)
        if d:
            nx = copy_to(t1.at[xx], c2.at[d], s2.at[d], r2.at[d], (x_peer(d), c))
            nx.start()
            second.append(nx)
    for cp in lefts:
        cp.wait_recv()
    total = gl_ref[c].astype(F32)
    for d in range(1, 8):
        total = total + cl[d].astype(F32)
    tl[...] = total.astype(BF16)
    backs = []
    for d in range(1, 8):
        cp = copy_to(tl, fl.at[c], s6.at[d], r6.at[d], (r, (c + d) % 8))
        cp.start()
        backs.append(cp)
    for cp in second:
        cp.wait_recv()
    third = []
    for d in (1, 2, 3, 0):
        zz = (z + d) % 4
        total = t1[x, zz].astype(F32)
        for n in range(1, 4):
            total = total + c2[n, zz].astype(F32)
        t2[zz] = total.astype(BF16)
        if d:
            cp = copy_to(t2.at[zz], c3.at[d], s3.at[d], r3.at[d], (z_peer(d), c))
            cp.start()
            third.append(cp)
    for cp in third:
        cp.wait_recv()
    total = t2[z].astype(F32)
    for n in range(1, 4):
        total = total + c3[n].astype(F32)
    t3[...] = total.astype(BF16)
    c4[c] = t3[64:96]

    def out_right(cc):
        return copy_to(t3.at[0:64], fr.at[piece], s4.at[cc], r4.at[piece], (owner, cc))

    for cc in range(8):

        @pl.when(jnp.logical_not((owner == r) & (c == cc)))
        def _():
            out_right(cc).start()

    @pl.when(owner == r)
    def _():
        fr[piece] = t3[0:64]

    maps = []
    for d in range(1, 8):
        cp = copy_to(t3.at[64:96], c4.at[c], s7.at[d], r7.at[d], (r, (c + d) % 8))
        cp.start()
        maps.append(cp)

    for cp in backs:
        cp.wait_recv()
    fl_ref[...] = fl[...]
    fl_ref[c] = tl[...]
    for cp in maps:
        cp.wait_recv()
    total = c4[0].astype(F32)
    for n in range(1, 8):
        total = total + c4[n].astype(F32)
    w_ref[...] = total.astype(BF16)
    for n in range(8):

        @pl.when(jnp.logical_not((source(n) == r) & (r // 4 == c)))
        def _():
            copy_to(fr.at[n], fr.at[n], s4.at[n], r4.at[n], (owner, c)).wait_recv()

    fr_ref[...] = fr[...]

    for _, _, cp in first:
        cp.wait_send()
    for cp in lefts + second + backs + third + maps:
        cp.wait_send()
    for cc in range(8):

        @pl.when(jnp.logical_not((owner == r) & (c == cc)))
        def _():
            out_right(cc).wait_send()


def reduce_all(sb, gl):
    vm = pl.BlockSpec(memory_space=pltpu.VMEM)
    sems = []
    for n in (4, 4, 4, 8, 8, 8, 8):
        sems += [pltpu.SemaphoreType.DMA((n,)), pltpu.SemaphoreType.DMA((n,))]
    return pl.pallas_call(
        reduce_kernel,
        out_shape=(
            jax.ShapeDtypeStruct((8, 64, 128), BF16),
            jax.ShapeDtypeStruct((8, 64, 128), BF16),
            jax.ShapeDtypeStruct((32, 128), BF16),
        ),
        in_specs=[vm] * 2,
        out_specs=(vm,) * 3,
        scratch_shapes=[
            pltpu.VMEM((4, 4, 96, 128), BF16),
            pltpu.VMEM((4, 4, 96, 128), BF16),
            pltpu.VMEM((4, 4, 96, 128), BF16),
            pltpu.VMEM((4, 96, 128), BF16),
            pltpu.VMEM((4, 96, 128), BF16),
            pltpu.VMEM((96, 128), BF16),
            pltpu.VMEM((8, 64, 128), BF16),
            pltpu.VMEM((8, 32, 128), BF16),
            pltpu.VMEM((8, 64, 128), BF16),
            pltpu.VMEM((64, 128), BF16),
            pltpu.VMEM((8, 64, 128), BF16),
            *sems,
        ],
        compiler_params=pltpu.CompilerParams(
            collective_id=1, has_side_effects=True, vmem_limit_bytes=32 << 20
        ),
        name="reduce_gradients",
    )(sb, gl)


def closing_kernel(x_ref, gain_ref, wt_ref, fl_ref, fr_ref, adj_ref, fac_ref, right, acc):
    right[...] = jnp.swapaxes(fr_ref[...].astype(F32), 0, 1)
    gain = gain_ref[...]
    wt = wt_ref[...]
    low = low_lanes((16, 128))
    acc[...] = jnp.zeros_like(acc)

    @pl.loop(0, 16)
    def _(m):
        x = x_ref[pl.ds(m * 2, 2)].astype(F32).reshape(128, 256)
        standard, inverse = normalise(x)
        normed = (standard * gain).astype(BF16)
        even, odd = right[2 * m], right[2 * m + 1]
        grads = jnp.concatenate(
            [
                fl_ref[pl.ds(pl.multiple_of(m * 32, 32), 32)],
                jnp.where(low, even, pltpu.roll(odd, 64, 1)).astype(BF16),
                jnp.where(low, pltpu.roll(even, 64, 1), odd).astype(BF16),
            ],
            axis=0,
        )
        acc[...] += mm(grads, normed)
        scaled = mm(grads, wt, TN) * gain
        mean = jnp.mean(scaled, -1, keepdims=True)
        along = jnp.mean(scaled * standard, -1, keepdims=True)
        adj = inverse * (scaled - mean - standard * along)
        adj_ref[pl.ds(m * 2, 2)] = adj.reshape(2, 64, 256)

    for n in range(8):
        fac_ref[n, 0:8] = acc[n * 8 : n * 8 + 8, 0:128]
        fac_ref[n, 8:16] = acc[n * 8 : n * 8 + 8, 128:256]


def closing(x, gain, wt, fl, fr):
    return pl.pallas_call(
        closing_kernel,
        out_shape=(
            jax.ShapeDtypeStruct((32, 64, 256), F32),
            jax.ShapeDtypeStruct((8, 16, 128), F32),
        ),
        scratch_shapes=[pltpu.VMEM((32, 16, 128), F32), pltpu.VMEM((64, 256), F32)],
        compiler_params=pltpu.CompilerParams(vmem_limit_bytes=32 << 20),
        name="closing",
    )(x, gain, wt, fl, fr)


def finish_kernel(
    fac_ref, bias_ref, w_ref, out_ref, ob_ref, wout_ref,
    b1, b2, b3, wz, wx, wc, s1, r1, s2, r2, s3, r3, s4, r4, s5, r5, s6, r6,
):
    r, c, z, x, core = place()
    sibling = (r + 1 - 2 * core, c)

    def plane(d):
        return z * 8 + (r + d) % 8

    def x_peer(d):
        return z * 8 + ((x + d) % 4) * 2 + core

    def z_peer(d):
        return ((z + d) % 4) * 8 + x * 2 + core

    barrier = pltpu.get_barrier_semaphore()
    for d in range(1, 8):
        for device in ((plane(d), c), (r, (c + d) % 8)):
            pl.semaphore_signal(barrier, inc=1, device_id=device, device_id_type=MESH)
    for d in range(1, 4):
        pl.semaphore_signal(barrier, inc=1, device_id=(z_peer(d), c), device_id_type=MESH)
    pl.semaphore_wait(barrier, 17)

    waits = []
    me = r % 8
    b1[me, 0:16] = fac_ref[c]
    b1[me, 16:24] = bias_ref[...]
    one = []
    for d in range(1, 8):
        cp = copy_to(b1.at[me], b1.at[me], s1.at[d], r1.at[d], (plane(d), c))
        cp.start()
        one.append(cp)
    wz[z] = w_ref[...]
    wone = []
    for d in range(1, 4):
        cp = copy_to(wz.at[z], wz.at[z], s4.at[d], r4.at[d], (z_peer(d), c))
        cp.start()
        wone.append(cp)
    for cp in one:
        cp.wait_recv()
    total = b1[0]
    for n in range(1, 8):
        total = total + b1[n]
    b2[z] = total
    two = []
    for d in range(1, 4):
        cp = copy_to(b2.at[z], b2.at[z], s2.at[d], r2.at[d], (z_peer(d), c))
        cp.start()
        two.append(cp)
    for cp in wone:
        cp.wait_recv()
    wx[x] = wz[...]
    wtwo = []
    for d in range(1, 4):
        cp = copy_to(wx.at[x], wx.at[x], s5.at[d], r5.at[d], (x_peer(d), c))
        cp.start()
        wtwo.append(cp)
    for cp in two:
        cp.wait_recv()
    total = b2[0]
    for n in range(1, 4):
        total = total + b2[n]
    b3[c] = total
    three = []
    for d in range(1, 8):
        cp = copy_to(b3.at[c], b3.at[c], s3.at[d], r3.at[d], (r, (c + d) % 8))
        cp.start()
        three.append(cp)
    for cp in wtwo:
        cp.wait_recv()
    wlast = copy_to(wx, wc, s6, r6, sibling)
    wlast.start()
    wout_ref[core] = wx[...]
    for cp in three:
        cp.wait_recv()
    bias = b3[0, 16:24]
    for n in range(1, 8):
        bias = bias + b3[n, 16:24]
    ob_ref[...] = bias
    out_ref[...] = b3[:, 0:16]
    wlast.wait_recv()
    wout_ref[1 - core] = wc[...]
    for cp in one + wone + two + wtwo + three:
        cp.wait_send()
    wlast.wait_send()


def finish(fac, bias, w):
    vm = pl.BlockSpec(memory_space=pltpu.VMEM)
    sems = []
    for n in (8, 4, 8, 4, 4):
        sems += [pltpu.SemaphoreType.DMA((n,)), pltpu.SemaphoreType.DMA((n,))]
    return pl.pallas_call(
        finish_kernel,
        out_shape=(
            jax.ShapeDtypeStruct((8, 16, 128), F32),
            jax.ShapeDtypeStruct((8, 128), F32),
            jax.ShapeDtypeStruct((2, 4, 4, 32, 128), BF16),
        ),
        in_specs=[vm] * 3,
        out_specs=(vm,) * 3,
        scratch_shapes=[
            pltpu.VMEM((8, 24, 128), F32),
            pltpu.VMEM((4, 24, 128), F32),
            pltpu.VMEM((8, 24, 128), F32),
            pltpu.VMEM((4, 32, 128), BF16),
            pltpu.VMEM((4, 4, 32, 128), BF16),
            pltpu.VMEM((4, 4, 32, 128), BF16),
            *sems,
            pltpu.SemaphoreType.DMA,
            pltpu.SemaphoreType.DMA,
        ],
        compiler_params=pltpu.CompilerParams(
            collective_id=2, has_side_effects=True, vmem_limit_bytes=32 << 20
        ),
        name="finish",
    )(fac, bias, w)


def per_device(
    sequence_stack,
    feature_multiplier,
    first_factor_map,
    second_factor_map,
    emitted_map,
    emitted_offset,
    upstream_adjoint,
):
    x = sequence_stack.transpose(1, 0, 2)
    gain = feature_multiplier.reshape(1, 256)
    wt = jnp.concatenate([first_factor_map.T, second_factor_map.T], axis=0)
    wp = emitted_map.reshape(32, 2, 4, 4, 128).transpose(2, 1, 3, 0, 4).reshape(1024, 128)
    wpt = wp.reshape(4, 256, 128).transpose(0, 2, 1)
    g = upstream_adjoint.reshape(4096, 128)

    la, lb, lt, rb = project(x, gain, wt)
    rt = gather(rb).reshape(2048, 128)
    lt = lt.reshape(64, 4, 256).transpose(1, 0, 2)
    pu, sb, gl, bias = sweep(la, lb, lt, rt, g, wp, wpt, emitted_offset.reshape(1, 128))
    fr, fl, w = reduce_all(sb, gl.reshape(8, 64, 128))
    adj, fac = closing(x, gain, wt, fl.reshape(512, 128), fr.reshape(16, 32, 128))
    fac, bias, w = finish(fac, bias, w)
    factor = fac.reshape(8, 2, 8, 128)
    factor = factor.transpose(0, 2, 1, 3).reshape(2, 32, 256).transpose(0, 2, 1)
    map_adjoint = w.reshape(32, 32, 128).transpose(1, 0, 2).reshape(1024, 128).astype(F32)
    return (
        pu.reshape(32, 128, 128),
        adj.transpose(1, 0, 2),
        factor,
        map_adjoint,
        jnp.sum(bias, 0),
    )


def solution(mesh):
    return jax.shard_map(
        per_device,
        mesh=mesh,
        in_specs=(P(None, "row", None), P(), P(), P(), P(), P(), P("row", "col", None)),
        out_specs=(P("row", "col", None), P(None, "row", None), P(), P(), P()),
        check_vma=False,
    )
```

time: 1180 us -> 112 us (0.09)
  waiting for transfers between devices: 705 us -> 0 us
  local copies, waits for them, and re-layouts: 199 us -> 7.39 us
  blocking collectives: 167 us -> 0 us
  Pallas kernels: 0 us -> 102 us
  matrix products: 55.8 us -> 0 us
  other arithmetic: 30.8 us -> 1.33 us
  between operations: 14.1 us -> 0.75 us
    psum x3 -> x0, waiting for transfers between devices: 603 us -> none  [the longest x1 246 us: per_device(): factor_maps_adjoint = lax.psum(factor_maps_share, 'row')]
    psum x2 -> x0, blocking collectives: 167 us -> none  [the longest x1 89.3 us: per_device(): lax.psum((left_part, right_mine), 'col')]
    pallas_call x0 -> x6, Pallas kernels: none -> 102 us  [the longest x1 31.4 us: reduce_all(): pl.pallas_call(reduce_kernel, out_shape=(jax.ShapeDtypeStruct((8, 64, 128...]
    all_gather x1 -> x0, waiting for transfers between devices: 102 us -> none  [per_device(): gathered = lax.all_gather(right, 'row', axis=1, tiled=True)]
    convert_element_type x16 -> x1, local copies, waits for them, and re-layouts: 83.4 us -> 1.1 us  [per_device(): w.reshape(32, 32, 128).transpose(1, 0, 2).reshape(1024, 128).astype(F32)]
    dot_general x30 -> x0, matrix products: 55.8 us -> none  [the longest x4 12.6 us: pair_block(): jnp.dot(outer.T, cot_rows, preferred_element_type=jnp.float32)]
    reshape x6 -> x1, local copies, waits for them, and re-layouts: 43.7 us -> 0.01 us  [per_device(): lt = lt.reshape(64, 4, 256).transpose(1, 0, 2)]
    transpose x4 -> x1, local copies, waits for them, and re-layouts: 23.7 us -> 1.05 us  [per_device(): emitted_map.reshape(32, 2, 4, 4, 128).transpose(2, 1, 3, 0, 4)]
  transfers between devices with their start and end apart: 4 -> 0, of which waited for: 4 -> 0; matrix products, arithmetic and copies ran while one was open for 2% -> 0% of each run, Pallas kernels for 0% -> 0%
where the time goes in v1:
time: 112 us; the launch traced here: 111 us
  Pallas kernels  102 us (91%)
  local copies, waits for them, and re-layouts  7.39 us (7%)
  other arithmetic  1.33 us (1%)
    pallas_call x1, Pallas kernels, reduce_all(): pl.pallas_call(reduce_kernel, out_shape=(jax.ShapeDtypeStruct((8, 64, 128...  31.4 us
    pallas_call x1, Pallas kernels, finish(): pl.pallas_call(finish_kernel, out_shape=(jax.ShapeDtypeStruct((8, 16, 128...  24 us
    pallas_call x1, Pallas kernels, sweep(): pl.pallas_call(sweep_kernel, out_shape=(jax.ShapeDtypeStruct((4096, 128),...  21.3 us
    pallas_call x1, Pallas kernels, gather(): pl.pallas_call(gather_kernel, out_shape=jax.ShapeDtypeStruct((16, 4, 32,...  14.3 us
    pallas_call x1, Pallas kernels, closing(): pl.pallas_call(closing_kernel, out_shape=(jax.ShapeDtypeStruct((32, 64, 2...  7.06 us
    unnamed x9, local copies, waits for them, and re-layouts  5.08 us
    pallas_call x1, Pallas kernels, project(): pl.pallas_call(project_kernel, out_shape=(jax.ShapeDtypeStruct((1024, 128...  3.9 us

profile of v1, /device:TPU:1, one launch (start us, length us, event | category | flops | bytes accessed | tf_op | source)
XLA Modules:
  0.0 111.5 jit_solution(11617785603247599246)
XLA Ops:
  0.6 0.0 copy-start.1
  0.6 0.7 pad_maximum_fusion.wt_ref
  1.4 1.1 copy.24
  2.4 0.1 copy.26
  2.6 0.0 copy-start
  2.6 0.0 copy-start.2
  2.6 1.9 %copy.32 = bf16[64,32,256]{2,0,1:T(8,128)(2,1)S(1)} copy(bf16[64,32,256]{2,1,0:T(8,128)(2,1)} %param.7) | data formatting | bytes 2097152 | tf_op args[0]
  4.5 0.0 copy-done.1
  4.5 3.9 %project.1 = (bf16[1024,128]{1,0:T(8,128)(2,1)S(1)}, bf16[1024,128]{1,0:T(8,128)(2,1)S(1)}, bf16[64,1024]{1,0:T(8,128)(2,1)S(1)}, bf16[16,32,128]{2,1,0:T(8,128)(2,1)S(1)}) custom-call(bf16[32,64,256]{2,1,0:T(8,128)(2,1)S(1)} %bitcast.40, f32[1,256]{1,0:T(1,128)S(1)} %bitcast.54, bf16[64,256]{1,0:T(8,128)(2,1)S(1)} %pad_maximum_fusion.wt_ref), custom_call_target="tpu_custom_call" | custom-call | tf_op jit(solution)/shard_map/project/pallas_call | solution.py:68
  8.4 14.3 %gather_right.1 = bf16[16,4,32,128]{3,2,1,0:T(8,128)(2,1)S(1)} custom-call(bf16[16,32,128]{2,1,0:T(8,128)(2,1)S(1)} %get-tuple-element.24.rb_ref), custom_call_target="tpu_custom_call" | custom-call | tf_op jit(solution)/shard_map/gather_right/pallas_call | solution.py:205
  22.8 0.0 copy-done
  22.8 0.0 copy-done.2
  22.8 21.3 %pair_sweep.1 = (bf16[4096,128]{1,0:T(8,128)(2,1)}, bf16[2,4,4,96,128]{4,3,2,1,0:T(8,128)(2,1)S(1)}, bf16[512,128]{1,0:T(8,128)(2,1)S(1)}, f32[8,128]{1,0:T(8,128)S(1)}) custom-call(bf16[1024,128]{1,0:T(8,128)(2,1)S(1)} %get-tuple-element.21.la_ref, bf16[1024,128]{1,0:T(8,128)(2,1)S(1)} %get-tuple-element.22.lb_ref, bf16[4,64,256]{2,1,0:T(8,128)(2,1)S(1)} %bitcast.48, ...), custom_call_target="tpu_custom_call" | custom-call | tf_op jit(solution)/shard_map/pair_sweep/pallas_call | solution.py:315
  44.1 31.4 %reduce_gradients.1 = (bf16[8,64,128]{2,1,0:T(8,128)(2,1)S(1)}, bf16[8,64,128]{2,1,0:T(8,128)(2,1)S(1)}, bf16[32,128]{1,0:T(8,128)(2,1)S(1)}) custom-call(bf16[2,4,4,96,128]{4,3,2,1,0:T(8,128)(2,1)S(1)} %get-tuple-element.26.sb_ref, bf16[8,64,128]{2,1,0:T(8,128)(2,1)S(1)} %bitcast.49), custom_call_target="tpu_custom_call" | custom-call | tf_op jit(solution)/shard_map/reduce_gradients/pallas_call | solution.py:489
  75.5 7.1 %closing.1 = (f32[32,64,256]{2,1,0:T(8,128)S(1)}, f32[8,16,128]{2,1,0:T(8,128)S(1)}) custom-call(bf16[32,64,256]{2,1,0:T(8,128)(2,1)S(1)} %bitcast.41, f32[1,256]{1,0:T(1,128)S(1)} %bitcast.55, bf16[64,256]{1,0:T(8,128)(2,1)S(1)} %pad_maximum_fusion.wt_ref, bf16[512,128]{1,0:T(8,128)(2,1)S(1)} %bitcast.51, bf16[16,32,128]{2,1,0:T(8,128)(2,1)S(1)} %bitcast.50), custom_call_target="tpu_custom_call" | custom-call | tf_op jit(solution)/shard_map/closing/pallas_call | solution.py:553
  82.5 2.5 %copy.28 = f32[64,32,256]{2,1,0:T(8,128)} copy(f32[64,32,256]{2,0,1:T(8,128)S(1)} %bitcast.44) | data formatting | bytes 4194304
  85.1 24.0 %finish.1 = (f32[8,16,128]{2,1,0:T(8,128)S(1)}, f32[8,128]{1,0:T(8,128)S(1)}, bf16[2,4,4,32,128]{4,3,2,1,0:T(8,128)(2,1)S(1)}) custom-call(f32[8,16,128]{2,1,0:T(8,128)S(1)} %get-tuple-element.31.fac_ref, f32[8,128]{1,0:T(8,128)S(1)} %get-tuple-element.32.bias_ref, bf16[32,128]{1,0:T(8,128)(2,1)S(1)} %get-tuple-element.33.w_ref), custom_call_target="tpu_custom_call" | custom-call | tf_op jit(solution)/shard_map/finish/pallas_call | solution.py:658
  109.1 0.5 reduce_sum.9
  109.6 0.1 convert_bitcast_fusion
  109.7 1.1 copy.27
  110.8 0.6 copy.35
  (1 shorter events, 0.0 us)
Async XLA Ops:
  0.6 3.9 %copy-start.1 = (f32[256]{0:T(256)S(1)}, f32[256]{0:T(256)}, u32[]{:S(2)}) copy-start(f32[256]{0:T(256)} %param.8) | copy-start | bytes 3076
  2.6 20.2 %copy-start = (bf16[32,128,128]{2,1,0:T(8,128)(2,1)S(1)}, bf16[32,128,128]{2,1,0:T(8,128)(2,1)}, u32[]{:S(2)}) copy-start(bf16[32,128,128]{2,1,0:T(8,128)(2,1)} %param.13) | copy-start | bytes 3145732
  2.6 20.2 %copy-start.2 = (f32[128]{0:T(128)S(1)}, f32[128]{0:T(128)}, u32[]{:S(2)}) copy-start(f32[128]{0:T(128)} %param.12) | copy-start | bytes 1540

commit v2 on v0

v2 whole, which is shorter than its diff:
```python
import jax
import jax.numpy as jnp
from jax import lax
from jax.experimental import pallas as pl
from jax.experimental.pallas import tpu as pltpu
from jax.sharding import PartitionSpec as P

MESH = pl.DeviceIdType.MESH
F32 = jnp.float32
BF16 = jnp.bfloat16
NN = (((1,), (0,)), ((), ()))
NT = (((1,), (1,)), ((), ()))
TN = (((0,), (0,)), ((), ()))


def mm(a, b, dims=NN):
    return lax.dot_general(a, b, dims, preferred_element_type=F32)


def low_lanes(shape):
    return lax.broadcasted_iota(jnp.int32, shape, 1) < 64


def normalise(x):
    average = jnp.mean(x, -1, keepdims=True)
    centered = x - average
    variance = jnp.mean(centered * centered, -1, keepdims=True)
    inverse = lax.rsqrt(variance + 1e-05)
    return centered * inverse, inverse


def place():
    r = lax.axis_index("row")
    return r, lax.axis_index("col"), r // 8, (r // 2) % 4, r % 2


def serving_half(z, x, z0, zh):
    gap = jnp.abs(z - z0)
    other = jnp.where(gap == 3, 1, jnp.where(gap == 2, (z + x) % 2, 0))
    return (zh + other) % 2


def copy_to(src, dst, send_sem, recv_sem, device):
    return pltpu.make_async_remote_copy(
        src_ref=src,
        dst_ref=dst,
        send_sem=send_sem,
        recv_sem=recv_sem,
        device_id=device,
        device_id_type=MESH,
    )


def unless(condition):
    return pl.when(jnp.logical_not(condition))


def kernel(
    x_ref, gain_ref, wt_ref, g_ref, wp_ref, wpt_ref, off_ref,
    pu_ref, adj_ref, fac_ref, bias_ref, map_ref,
    la, lb, lt, left, right, rb, land, dt, ot, glx,
    sr, cr1, tr1, cr2, tr2, cr3, tr3, fr,
    sw, cw1, tw1, cw2, tw2, cw3, cw4, wz, wx, wc,
    cl, tl, fl, bias, closing, acc, fs, fc1, fx, fz, ff,
    gs, gd, ks, kd, own_sem,
    s1, r1, s2, r2, s3, r3, s4, r4, s5, r5, s6, r6, s7, r7, s8, r8, s9, r9,
    s10, r10, s11, r11, s12, r12, s13, r13, s14, r14, s15, r15, s16, r16,
):
    r, c, z, x, core = place()
    zh, y = c // 4, c % 4
    sibling = (r + 1 - 2 * core, c)
    goal = r // 4
    k = core + 2 * (z // 2)
    owner = 4 * c + k
    piece = x * 2 + z % 2

    def x_row(xx):
        return z * 8 + xx * 2 + core

    def z_row(zz):
        return zz * 8 + x * 2 + core

    def giver(m, q):
        row = 4 * c + core + 2 * m
        return row, serving_half(z, x, row // 8, zh) * 4 + q

    def source(n):
        return (((r % 4) // 2) * 2 + n % 2) * 8 + (n // 2) * 2 + r % 2

    def chip(step):
        dz, dx = (z + step // 4) % 4, (x + step % 4) % 4
        serves = serving_half(dz, dx, z, goal // 4) == zh
        return dz, dx, serves, (goal == c) & (step == 0)

    barrier = pltpu.get_barrier_semaphore()

    def signal(device):
        pl.semaphore_signal(barrier, inc=1, device_id=device, device_id_type=MESH)

    signal(sibling)
    for d in range(1, 4):
        signal((x_row((x + d) % 4), c))
        signal((z_row((z + d) % 4), c))
    for d in range(1, 8):
        signal((r, (c + d) % 8))
    for n in range(8):

        @unless((source(n) == r) & (goal == c))
        def _():
            signal((source(n), goal))

        row, col = giver(n % 2, n // 2)

        @unless((row == r) & (col == c))
        def _():
            signal((row, col))

    gain = gain_ref[...]
    wt = wt_ref[...]
    low32 = low_lanes((32, 128))
    low16 = low_lanes((16, 128))

    @pl.loop(0, 8)
    def _(b):
        xs = x_ref[pl.ds(b * 4, 4)].astype(F32).reshape(256, 256)
        standard, _ = normalise(xs)
        normed = (standard * gain).astype(BF16)
        both = mm(wt, normed, NT).astype(BF16).astype(F32)
        for p in range(2):
            tile = both[:, p * 128 : (p + 1) * 128]
            turned = pltpu.roll(tile, 64, 1)
            row = pl.multiple_of(b * 128 + p * 64, 64)
            scaled, scaled_turned = tile[:32] * (1 / 64), turned[:32] * (1 / 64)
            zero = jnp.zeros_like(scaled)
            la[pl.ds(row, 32)] = jnp.where(low32, scaled, zero).astype(BF16)
            lb[pl.ds(row, 32)] = jnp.where(low32, zero, scaled_turned).astype(BF16)
            la[pl.ds(row + 32, 32)] = jnp.where(low32, scaled_turned, zero).astype(BF16)
            lb[pl.ds(row + 32, 32)] = jnp.where(low32, zero, scaled).astype(BF16)
            left[pl.ds(row, 32)] = scaled
            left[pl.ds(row + 32, 32)] = scaled_turned
            j = b * 4 + p * 2
            right[j] = jnp.where(low16, tile[32:48], turned[48:64])
            right[j + 1] = jnp.where(low16, turned[32:48], tile[48:64])

    rb[...] = jnp.swapaxes(right[...], 0, 1).astype(BF16)

    count = jnp.int32(14 + 8) - jnp.where(owner == r, 1, 0)
    for step in range(16):
        dz, dx, serves, myself = chip(step)
        count = count + jnp.where(serves & jnp.logical_not(myself), 1, 0)
    pl.semaphore_wait(barrier, count)

    mine = rb.at[pl.ds(y * 4, 4)]
    slot = land.at[pl.ds(y * 4, 4), r % 4]

    def give(step):
        dz, dx, serves, myself = chip(step)
        cp = copy_to(
            mine, slot, gs.at[step], gd.at[((r % 4) // 2) * 4 + y], (dz * 8 + dx * 2 + core, goal)
        )
        return serves & jnp.logical_not(myself), cp

    for step in range(16):
        sends, cp = give(step)

        @pl.when(sends)
        def _():
            cp.start()

    @pl.when((goal == c) & (chip(0)[2]))
    def _():
        own = pltpu.make_async_copy(mine, slot, own_sem)
        own.start()
        own.wait()

    for b in range(8):
        lt[:, b * 128 : (b + 1) * 128] = left[b * 128 : (b + 1) * 128].T[:64].astype(BF16)

    def core_right(q):
        return copy_to(sr.at[1 - core, q], cr1.at[q], s1.at[q], r1.at[q], sibling)

    def x_right(q):
        return copy_to(tr1.at[q], cr2.at[x], s2.at[q], r2.at[x], (x_row(q), c))

    def pass_right(q):
        core_right(q).wait_recv()
        tr1[q] = (sr[core, q].astype(F32) + cr1[q].astype(F32)).astype(BF16)

        @pl.when(x != q)
        def _():
            x_right(q).start()

    @pl.loop(0, 4)
    def _(q):
        wq = wp_ref[pl.ds(pl.multiple_of(q * 256, 256), 256)]

        @pl.loop(0, 4)
        def _(b):
            g = g_ref[pl.ds(pl.multiple_of(b * 1024, 1024), 1024)]
            d = mm(wq, g, NT).astype(BF16)
            for e in range(8):
                for i in range(8):
                    dt[
                        pl.ds(pl.multiple_of(b * 256 + i * 32, 32), 32),
                        pl.ds(pl.multiple_of(q * 1024 + e * 128, 128), 128),
                    ] = d[e * 32 : e * 32 + 32, i * 128 : i * 128 + 128]

        gr = mm(lt[...], dt[:, pl.ds(pl.multiple_of(q * 1024, 1024), 1024)])
        for e1 in range(4):
            tile = jnp.concatenate(
                [gr[:, e1 * 128 : e1 * 128 + 128], gr[:, 512 + e1 * 128 : 640 + e1 * 128]], axis=0
            )
            turned = tile.T.astype(BF16)
            for kk in range(4):
                at = (e1 % 2) * 32
                sr[kk % 2, q, (kk // 2) * 2 + e1 // 2, at : at + 32] = turned[kk * 32 : kk * 32 + 32]
        core_right(q).start()

        @pl.when(q > 0)
        def _():
            pass_right(q - 1)

    def swap(q, m):
        there = land.at[pl.ds(q * 4, 4), core + 2 * m]
        return copy_to(there, there, ks.at[m * 4 + q], kd.at[m * 4 + q], sibling)

    for q in range(4):
        for m in range(2):
            row, col = giver(m, q)
            there = land.at[pl.ds(q * 4, 4), core + 2 * m]

            @unless((row == r) & (col == c))
            def _():
                copy_to(there, there, ks.at[m * 4 + q], gd.at[m * 4 + q], sibling).wait_recv()

            swap(q, m).start()
    pass_right(3)
    for q in range(4):
        for m in range(2):
            there = land.at[pl.ds(q * 4, 4), 1 - core + 2 * m]
            copy_to(there, there, ks.at[m * 4 + q], kd.at[m * 4 + q], sibling).wait_recv()

    bias[...] = jnp.zeros_like(bias)

    @pl.loop(0, 4)
    def _(b):
        rows = pl.ds(pl.multiple_of(b * 256, 256), 256)
        first = jnp.zeros((256, 128), F32)
        second = jnp.zeros((256, 128), F32)
        for q in range(4):
            part = land[q * 4 : q * 4 + 4].reshape(512, 128)
            first = first + mm(dt[rows, q * 1024 : q * 1024 + 512], part)
            second = second + mm(dt[rows, q * 1024 + 512 : q * 1024 + 1024], part)
        for m in range(4):
            even, odd = slice(m * 64, m * 64 + 32), slice(m * 64 + 32, m * 64 + 64)
            one = first[even] + pltpu.roll(second[even], 64, 1)
            two = second[odd] + pltpu.roll(first[odd], 64, 1)
            at = (m % 2) * 32
            glx[b * 2 + m // 2, at : at + 32] = (jnp.where(low32, one, two) * (1 / 64)).astype(BF16)
        g = g_ref[pl.ds(pl.multiple_of(b * 1024, 1024), 1024)]
        bias[...] += jnp.sum(g.astype(F32).reshape(64, 16, 128), 0)

    for n in range(8):
        glx[n, 64:80] = bias[...].astype(BF16)
    lefts = []
    for d in range(1, 8):
        cc = (c + d) % 8
        lefts.append(copy_to(glx.at[cc], cl.at[c], s5.at[d], r5.at[d], (r, cc)))
        lefts[-1].start()

    def core_map(q):
        return copy_to(sw.at[1 - core, q], cw1.at[q], s7.at[q], r7.at[q], sibling)

    def x_map(q):
        return copy_to(tw1.at[q], cw2.at[x], s8.at[q], r8.at[x], (x_row(q), c))

    def pass_map(q):
        core_map(q).wait_recv()
        tw1[q] = (sw[core, q].astype(F32) + cw1[q].astype(F32)).astype(BF16)

        @pl.when(x != q)
        def _():
            x_map(q).start()

    def z_right(d):
        zz = (z + d) % 4
        return copy_to(tr2.at[zz], cr3.at[d], s3.at[d], r3.at[d], (z_row(zz), c))

    def out_right(cc):
        return copy_to(tr3, fr.at[piece], s4.at[cc], r4.at[piece], (owner, cc))

    def out_left(d):
        return copy_to(tl, fl.at[c], s6.at[d], r6.at[d], (r, (c + d) % 8))

    @pl.loop(0, 4)
    def _(q):
        part = land[pl.ds(q * 4, 4)].reshape(512, 128)

        @pl.loop(0, 4)
        def _(b):
            rows = pl.ds(pl.multiple_of(b * 256, 256), 256)
            for e2, l in enumerate((la, lb)):
                o = mm(l[rows], part, NT).astype(BF16)
                for e1 in range(4):
                    for i in range(8):
                        ot[
                            pl.ds(pl.multiple_of(q * 256 + (e2 * 4 + e1) * 32, 32), 32),
                            pl.ds(pl.multiple_of(b * 1024 + i * 128, 128), 128),
                        ] = o[i * 32 : i * 32 + 32, e1 * 128 : e1 * 128 + 128]

        gw = mm(ot[pl.ds(pl.multiple_of(q * 256, 256), 256)], g_ref[...])
        for cc in range(2):
            for zz in range(4):
                at = cc * 128 + zz * 32
                sw[cc, q, zz] = gw[at : at + 32].astype(BF16)
        core_map(q).start()

        @pl.when(q > 0)
        def _():
            pass_map(q - 1)

        @pl.when(q == 1)
        def _():
            for d in range(1, 4):
                n = (x + d) % 4
                copy_to(cr2.at[n], cr2.at[n], s2.at[0], r2.at[n], sibling).wait_recv()
            for d in (1, 2, 3, 0):
                zz = (z + d) % 4
                total = tr1[x, zz].astype(F32)
                for n in range(1, 4):
                    total = total + cr2[(x + n) % 4, zz].astype(F32)
                tr2[zz] = total.astype(BF16)
                if d:
                    z_right(d).start()

        @pl.when(q == 2)
        def _():
            for cp in lefts:
                cp.wait_recv()
            cl[c] = glx[c]
            total = cl[0].astype(F32)
            for n in range(1, 8):
                total = total + cl[n].astype(F32)
            tl[...] = total[:64].astype(BF16)
            bias[...] = total[64:]
            for d in range(1, 8):
                out_left(d).start()

        @pl.when(q == 3)
        def _():
            for d in range(1, 4):
                z_right(d).wait_recv()
            total = tr2[z].astype(F32)
            for n in range(1, 4):
                total = total + cr3[n].astype(F32)
            tr3[...] = total.astype(BF16)
            for cc in range(8):

                @unless((owner == r) & (c == cc))
                def _():
                    out_right(cc).start()

            @pl.when(owner == r)
            def _():
                fr[piece] = tr3[...]

    def z_map(d):
        zz = (z + d) % 4
        return copy_to(tw2.at[zz], cw3.at[d], s9.at[d], r9.at[d], (z_row(zz), c))

    def col_map(d):
        return copy_to(cw4.at[c], cw4.at[c], s10.at[d], r10.at[d], (r, (c + d) % 8))

    offset = off_ref[...]

    @pl.loop(0, 4)
    def _(b):
        update = mm(wpt_ref[...], ot[:, pl.ds(pl.multiple_of(b * 1024, 1024), 1024)])
        for i in range(8):
            at = pl.multiple_of(b * 1024 + i * 128, 128)
            pu_ref[pl.ds(at, 128)] = (update[:, i * 128 : i * 128 + 128].T + offset).astype(BF16)

        @pl.when(b == 0)
        def _():
            pass_map(3)

        @pl.when(b == 3)
        def _():
            for d in range(1, 4):
                n = (x + d) % 4
                copy_to(cw2.at[n], cw2.at[n], s8.at[0], r8.at[n], sibling).wait_recv()
            for d in (1, 2, 3, 0):
                zz = (z + d) % 4
                total = tw1[x, zz].astype(F32)
                for n in range(1, 4):
                    total = total + cw2[(x + n) % 4, zz].astype(F32)
                tw2[zz] = total.astype(BF16)
                if d:
                    z_map(d).start()

    for d in range(1, 8):
        out_left(d).wait_recv()
    fl[c] = tl[...]
    for n in range(8):

        @unless((source(n) == r) & (goal == c))
        def _():
            copy_to(fr.at[n], fr.at[n], s4.at[n], r4.at[n], sibling).wait_recv()

    for d in range(1, 4):
        z_map(d).wait_recv()
    total = tw2[z].astype(F32)
    for n in range(1, 4):
        total = total + cw3[n].astype(F32)
    cw4[c] = total.astype(BF16)
    for d in range(1, 8):
        col_map(d).start()

    closing[...] = jnp.swapaxes(fr[...].reshape(16, 32, 128).astype(F32), 0, 1)
    acc[...] = jnp.zeros_like(acc)

    @pl.loop(0, 16)
    def _(m):
        xs = x_ref[pl.ds(m * 2, 2)].astype(F32).reshape(128, 256)
        standard, inverse = normalise(xs)
        normed = (standard * gain).astype(BF16)
        even, odd = closing[2 * m], closing[2 * m + 1]
        grads = jnp.concatenate(
            [
                fl[m // 2, pl.ds(pl.multiple_of((m % 2) * 32, 32), 32)],
                jnp.where(low16, even, pltpu.roll(odd, 64, 1)).astype(BF16),
                jnp.where(low16, pltpu.roll(even, 64, 1), odd).astype(BF16),
            ],
            axis=0,
        )
        acc[...] += mm(grads, normed)
        scaled = mm(grads, wt, TN) * gain
        mean = jnp.mean(scaled, -1, keepdims=True)
        along = jnp.mean(scaled * standard, -1, keepdims=True)
        adj = inverse * (scaled - mean - standard * along)
        adj_ref[pl.ds(m * 2, 2)] = adj.reshape(2, 64, 256)

    for n in range(2):
        for h in range(2):
            at = h * 32
            fs[n, at : at + 32] = acc[n * 32 : n * 32 + 32, h * 128 : h * 128 + 128]
        fs[n, 64:80] = bias[...]
    half = copy_to(fs.at[1 - core], fc1, s11.at[0], r11.at[0], sibling)
    half.start()
    for d in range(1, 8):
        col_map(d).wait_recv()
    total = cw4[0].astype(F32)
    for n in range(1, 8):
        total = total + cw4[n].astype(F32)
    wz[z] = total.astype(BF16)
    zs = [
        copy_to(wz.at[z], wz.at[z], s12.at[d], r12.at[d], (z_row((z + d) % 4), c)) for d in range(1, 4)
    ]
    for cp in zs:
        cp.start()
    half.wait_recv()
    fx[x] = (fs[core] + fc1[...]).astype(BF16)
    fxs = [
        copy_to(fx.at[x], fx.at[x], s13.at[d], r13.at[d], (x_row((x + d) % 4), c)) for d in range(1, 4)
    ]
    for cp in fxs:
        cp.start()
    for cp in zs:
        cp.wait_recv()
    wx[x] = wz[...]
    xs_ = [
        copy_to(wx.at[x], wx.at[x], s14.at[d], r14.at[d], (x_row((x + d) % 4), c)) for d in range(1, 4)
    ]
    for cp in xs_:
        cp.start()
    for cp in fxs:
        cp.wait_recv()
    total = fx[0].astype(F32)
    for n in range(1, 4):
        total = total + fx[n].astype(F32)
    fz[z] = total.astype(BF16)
    fzs = [
        copy_to(fz.at[z], fz.at[z], s15.at[d], r15.at[d], (z_row((z + d) % 4), c)) for d in range(1, 4)
    ]
    for cp in fzs:
        cp.start()
    for cp in xs_:
        cp.wait_recv()
    last = copy_to(wx, wc, s16.at[0], r16.at[0], sibling)
    last.start()
    map_ref[core] = wx[...]
    for cp in fzs:
        cp.wait_recv()
    total = fz[0].astype(F32)
    for n in range(1, 4):
        total = total + fz[n].astype(F32)
    ff[core] = total[:64]
    end = copy_to(ff.at[core], ff.at[core], s11.at[1], r11.at[1], sibling)
    end.start()
    bias_ref[...] = total[64:]
    last.wait_recv()
    map_ref[1 - core] = wc[...]
    end.wait_recv()
    fac_ref[...] = ff[...]

    for step in range(16):
        sends, cp = give(step)

        @pl.when(sends)
        def _():
            cp.wait_send()

    for q in range(4):
        core_right(q).wait_send()
        core_map(q).wait_send()

        @pl.when(x != q)
        def _():
            x_right(q).wait_send()
            x_map(q).wait_send()

        for m in range(2):
            swap(q, m).wait_send()
    for d in range(1, 4):
        z_right(d).wait_send()
        z_map(d).wait_send()
    for d in range(1, 8):
        out_left(d).wait_send()
        col_map(d).wait_send()
    for cc in range(8):

        @unless((owner == r) & (c == cc))
        def _():
            out_right(cc).wait_send()

    for cp in lefts + zs + fxs + xs_ + fzs + [half, last, end]:
        cp.wait_send()


def run(x, gain, wt, g, wp, wpt, off):
    vm = pl.BlockSpec(memory_space=pltpu.VMEM)

    def b16(*shape):
        return pltpu.VMEM(shape, BF16)

    def f32(*shape):
        return pltpu.VMEM(shape, F32)

    sems = []
    for n in (4, 4, 4, 8, 8, 8, 4, 4, 4, 8, 2, 4, 4, 4, 4, 1):
        sems += [pltpu.SemaphoreType.DMA((n,)), pltpu.SemaphoreType.DMA((n,))]
    return pl.pallas_call(
        kernel,
        out_shape=(
            jax.ShapeDtypeStruct((4096, 128), BF16),
            jax.ShapeDtypeStruct((32, 64, 256), F32),
            jax.ShapeDtypeStruct((2, 64, 128), F32),
            jax.ShapeDtypeStruct((16, 128), F32),
            jax.ShapeDtypeStruct((2, 4, 4, 32, 128), BF16),
        ),
        in_specs=[vm] * 7,
        out_specs=(vm,) * 5,
        scratch_shapes=[
            b16(1024, 128), b16(1024, 128), b16(64, 1024), f32(1024, 128), f32(32, 16, 128),
            b16(16, 32, 128), b16(16, 4, 32, 128), b16(1024, 4096), b16(1024, 4096), b16(8, 80, 128),
            b16(2, 4, 4, 64, 128), b16(4, 4, 64, 128), b16(4, 4, 64, 128), b16(4, 4, 64, 128),
            b16(4, 64, 128), b16(4, 64, 128), b16(64, 128), b16(8, 64, 128),
            b16(2, 4, 4, 32, 128), b16(4, 4, 32, 128), b16(4, 4, 32, 128), b16(4, 4, 32, 128),
            b16(4, 32, 128), b16(4, 32, 128), b16(8, 32, 128), b16(4, 32, 128), b16(4, 4, 32, 128),
            b16(4, 4, 32, 128),
            b16(8, 80, 128), b16(64, 128), b16(8, 64, 128), f32(16, 128), f32(32, 16, 128), f32(64, 256),
            f32(2, 80, 128), f32(80, 128), b16(4, 80, 128), b16(4, 80, 128), f32(2, 64, 128),
            pltpu.SemaphoreType.DMA((16,)), pltpu.SemaphoreType.DMA((8,)),
            pltpu.SemaphoreType.DMA((8,)), pltpu.SemaphoreType.DMA((8,)), pltpu.SemaphoreType.DMA,
            *sems,
        ],
        compiler_params=pltpu.CompilerParams(
            collective_id=0, has_side_effects=True, vmem_limit_bytes=56 << 20
        ),
        name="outer_product_mean",
    )(x, gain, wt, g, wp, wpt, off)


def per_device(
    sequence_stack,
    feature_multiplier,
    first_factor_map,
    second_factor_map,
    emitted_map,
    emitted_offset,
    upstream_adjoint,
):
    x = sequence_stack.transpose(1, 0, 2)
    wt = jnp.concatenate([first_factor_map.T, second_factor_map.T], axis=0)
    wp = emitted_map.reshape(32, 2, 4, 4, 128).transpose(2, 1, 3, 0, 4).reshape(1024, 128)
    pu, adj, fac, bias, w = run(
        x,
        feature_multiplier.reshape(1, 256),
        wt,
        upstream_adjoint.reshape(4096, 128),
        wp,
        wp.T,
        emitted_offset.reshape(1, 128),
    )
    factor = fac.reshape(2, 2, 32, 128).transpose(0, 2, 1, 3).reshape(2, 32, 256).transpose(0, 2, 1)
    return (
        pu.reshape(32, 128, 128),
        adj.transpose(1, 0, 2),
        factor,
        w.reshape(32, 32, 128).transpose(1, 0, 2).reshape(1024, 128).astype(F32),
        jnp.sum(bias, 0),
    )


def solution(mesh):
    return jax.shard_map(
        per_device,
        mesh=mesh,
        in_specs=(P(None, "row", None), P(), P(), P(), P(), P(), P("row", "col", None)),
        out_specs=(P("row", "col", None), P(None, "row", None), P(), P(), P()),
        check_vma=False,
    )
```

time: 1180 us -> 82.9 us (0.07)
  waiting for transfers between devices: 705 us -> 0 us
  local copies, waits for them, and re-layouts: 199 us -> 11.6 us
  blocking collectives: 167 us -> 0 us
  Pallas kernels: 0 us -> 68.2 us
  matrix products: 55.8 us -> 0 us
  other arithmetic: 30.8 us -> 1.94 us
  between operations: 14.1 us -> 0.7 us
    psum x3 -> x0, waiting for transfers between devices: 603 us -> none  [the longest x1 246 us: per_device(): factor_maps_adjoint = lax.psum(factor_maps_share, 'row')]
    psum x2 -> x0, blocking collectives: 167 us -> none  [the longest x1 89.3 us: per_device(): lax.psum((left_part, right_mine), 'col')]
    all_gather x1 -> x0, waiting for transfers between devices: 102 us -> none  [per_device(): gathered = lax.all_gather(right, 'row', axis=1, tiled=True)]
    convert_element_type x16 -> x1, local copies, waits for them, and re-layouts: 83.4 us -> 1.1 us  [per_device(): w.reshape(32, 32, 128).transpose(1, 0, 2).reshape(1024, 128).astype(F32)]
    pallas_call x0 -> x1, Pallas kernels: none -> 68.2 us  [run(): pl.pallas_call(kernel, out_shape=(jax.ShapeDtypeStruct((4096, 128), BF16)...]
    dot_general x30 -> x0, matrix products: 55.8 us -> none  [the longest x4 12.6 us: pair_block(): jnp.dot(outer.T, cot_rows, preferred_element_type=jnp.float32)]
    reshape x6 -> x2, local copies, waits for them, and re-layouts: 43.7 us -> 1.48 us  [the longest x1 0.85 us: per_device(): emitted_map.reshape(32, 2, 4, 4, 128).transpose(2, 1, 3, 0, 4)]
    transpose x4 -> x1, local copies, waits for them, and re-layouts: 23.7 us -> 1.05 us  [per_device(): emitted_map.reshape(32, 2, 4, 4, 128).transpose(2, 1, 3, 0, 4)]
  transfers between devices with their start and end apart: 4 -> 0, of which waited for: 4 -> 0; matrix products, arithmetic and copies ran while one was open for 2% -> 0% of each run, Pallas kernels for 0% -> 0%
where the time goes in v2:
time: 82.9 us; the launch traced here: 82.5 us
  Pallas kernels  68.2 us (82%)
  local copies, waits for them, and re-layouts  11.6 us (14%)
  other arithmetic  1.94 us (2%)
    pallas_call x1, Pallas kernels, run(): pl.pallas_call(kernel, out_shape=(jax.ShapeDtypeStruct((4096, 128), BF16)...  68.2 us
    unnamed x13, local copies, waits for them, and re-layouts  8 us

profile of v2, /device:TPU:1, one launch (start us, length us, event | category | flops | bytes accessed | tf_op | source)
XLA Modules:
  0.0 82.5 jit_solution(4969623314993804941)
XLA Ops:
  0.6 1.4 %pad_maximum_fusion.wt_ref = bf16[64,256]{1,0:T(8,128)(2,1)} fusion(bf16[32,256]{1,0:T(8,128)(2,1)} %bitcast.42, bf16[32,256]{1,0:T(8,128)(2,1)} %bitcast.43), kind=kLoop, calls=%fused_computation.3 | loop fusion | flops 65536 | bytes 65536 | tf_op jit(solution)/shard_map/concatenate | solution.py:594
  2.0 1.1 %copy.24 = bf16[4,2,4,32,128]{4,3,2,1,0:T(8,128)(2,1)S(1)} copy(bf16[4,2,4,32,128]{4,2,0,1,3:T(4,128)(2,1)} %bitcast.39) | data formatting | bytes 524288 | tf_op jit(solution)/shard_map/transpose | solution.py:595
  3.0 0.0 copy-start
  3.1 0.9 %copy.25 = bf16[1024,128]{0,1:T(8,128)(2,1)} copy(bf16[1024,128]{1,0:T(8,128)(2,1)S(1)} %bitcast.32) | data formatting | bytes 524288 | tf_op jit(solution)/shard_map/reshape | solution.py:595
  3.9 2.8 %copy.32 = bf16[64,32,256]{2,0,1:T(8,128)(2,1)} copy(bf16[64,32,256]{2,1,0:T(8,128)(2,1)} %param.7) | data formatting | bytes 2097152 | tf_op args[0]
  6.7 0.0 copy-done
  6.7 68.2 %outer_product_mean.1 = (bf16[4096,128]{1,0:T(8,128)(2,1)}, f32[32,64,256]{2,1,0:T(8,128)}, f32[2,64,128]{2,1,0:T(8,128)}, f32[16,128]{1,0:T(8,128)}, bf16[2,4,4,32,128]{4,3,2,1,0:T(8,128)(2,1)}) custom-call(bf16[32,64,256]{2,1,0:T(8,128)(2,1)} %bitcast.31, f32[1,256]{1,0:T(1,128)} %bitcast.44, bf16[64,256]{1,0:T(8,128)(2,1)} %pad_maximum_fusion.wt_ref, ...), custom_call_target="tpu_custom_call" | custom-call | tf_op jit(solution)/shard_map/outer_product_mean/pallas_call | solution.py:552
  74.9 0.0 copy-start.4
  74.9 0.0 copy-start.3
  74.9 0.0 copy-start.2
  74.9 0.0 copy-start.1
  74.9 4.2 %copy.28 = f32[64,32,256]{2,1,0:T(8,128)} copy(f32[64,32,256]{2,0,1:T(8,128)} %bitcast.34) | data formatting | bytes 4194304
  79.2 0.0 copy-done.4
  79.2 0.5 reduce_sum.9
  79.7 0.0 copy-done.3
  79.7 0.6 copy.33
  80.3 0.0 copy-done.2
  80.4 0.1 convert_bitcast_fusion
  80.4 1.1 %copy.27 = f32[32,32,128]{2,1,0:T(8,128)} copy(f32[32,32,128]{2,0,1:T(8,128)S(1)} %convert_bitcast_fusion) | data formatting | bytes 1048576 | tf_op jit(solution)/shard_map/convert_element_type | solution.py:610
  81.5 0.0 copy-done.1
  81.5 1.0 %copy.35 = bf16[32,128,128]{2,1,0:T(8,128)(2,1)} copy(bf16[32,128,128]{2,1,0:T(8,128)(2,1)S(1)} %bitcast.36) | data formatting | bytes 2097152
Async XLA Ops:
  3.0 3.6 %copy-start = (bf16[4,2,4,32,128]{4,3,2,1,0:T(8,128)(2,1)}, bf16[4,2,4,32,128]{4,3,2,1,0:T(8,128)(2,1)S(1)}, u32[]{:S(2)}) copy-start(bf16[4,2,4,32,128]{4,3,2,1,0:T(8,128)(2,1)S(1)} %copy.24) | copy-start | bytes 786436
  74.9 4.3 %copy-start.4 = (f32[16,128]{1,0:T(8,128)S(1)}, f32[16,128]{1,0:T(8,128)}, u32[]{:S(2)}) copy-start(f32[16,128]{1,0:T(8,128)} %get-tuple-element.14) | copy-start | bytes 24580
  74.9 4.8 %copy-start.3 = (f32[2,64,128]{2,1,0:T(8,128)S(1)}, f32[2,64,128]{2,1,0:T(8,128)}, u32[]{:S(2)}) copy-start(f32[2,64,128]{2,1,0:T(8,128)} %get-tuple-element.12) | copy-start | bytes 196612
  74.9 5.4 %copy-start.2 = (bf16[2,4,4,32,128]{4,3,2,1,0:T(8,128)(2,1)S(1)}, bf16[2,4,4,32,128]{4,3,2,1,0:T(8,128)(2,1)}, u32[]{:S(2)}) copy-start(bf16[2,4,4,32,128]{4,3,2,1,0:T(8,128)(2,1)} %get-tuple-element.13) | copy-start | bytes 786436
  74.9 6.6 %copy-start.1 = (bf16[4096,128]{1,0:T(8,128)(2,1)S(1)}, bf16[4096,128]{1,0:T(8,128)(2,1)}, u32[]{:S(2)}) copy-start(bf16[4096,128]{1,0:T(8,128)(2,1)} %get-tuple-element.10) | copy-start | bytes 3145732

commit v3 on v2

--- a/solution.py
+++ b/solution.py
@@ -56,13 +56,14 @@
 
 
 def kernel(
-    x_ref, gain_ref, wt_ref, g_ref, wp_ref, wpt_ref, off_ref,
-    pu_ref, adj_ref, fac_ref, bias_ref, map_ref,
+    x_ref, gain_ref, w1_ref, w2_ref, g_hbm, w_ref, off_ref,
+    pu_hbm, adj_hbm, fac_ref, bias_ref, map_ref,
+    st, inv, g_ref, wt_ref, wp_ref, wpt_ref, pu_ref, turn, adj_ref,
     la, lb, lt, left, right, rb, land, dt, ot, glx,
     sr, cr1, tr1, cr2, tr2, cr3, tr3, fr,
     sw, cw1, tw1, cw2, tw2, cw3, cw4, wz, wx, wc,
-    cl, tl, fl, bias, closing, acc, fs, fc1, fx, fz, ff,
-    gs, gd, ks, kd, own_sem,
+    cl, tl, fl, bias, closing, acc, grads_all, tall, fs, fc1, fx, fz, ff,
+    gs, gd, ks, kd, own_sem, g_sem, pu_sem, adj_sem,
     s1, r1, s2, r2, s3, r3, s4, r4, s5, r5, s6, r6, s7, r7, s8, r8, s9, r9,
     s10, r10, s11, r11, s12, r12, s13, r13, s14, r14, s15, r15, s16, r16,
 ):
@@ -115,15 +116,28 @@
         def _():
             signal((row, col))
 
+    bring = pltpu.make_async_copy(g_hbm, g_ref, g_sem)
+    bring.start()
+
     gain = gain_ref[...]
-    wt = wt_ref[...]
+    wt = jnp.concatenate([w1_ref[...], w2_ref[...]], axis=0)
+    wt_ref[...] = wt
+
+    @pl.loop(0, 8)
+    def _(b):
+        rows = pl.ds(pl.multiple_of(b * 8, 8), 8)
+        for h in range(2):
+            xs = x_ref[rows, h * 16 : h * 16 + 16].astype(F32)
+            st[h * 16 : h * 16 + 16, rows] = jnp.swapaxes(xs, 0, 1)
+
     low32 = low_lanes((32, 128))
     low16 = low_lanes((16, 128))
 
     @pl.loop(0, 8)
     def _(b):
-        xs = x_ref[pl.ds(b * 4, 4)].astype(F32).reshape(256, 256)
-        standard, _ = normalise(xs)
+        standard, inverse = normalise(st[pl.ds(b * 4, 4)].reshape(256, 256))
+        st[pl.ds(b * 4, 4)] = standard.reshape(4, 64, 256)
+        inv[pl.ds(b * 4, 4)] = inverse.reshape(4, 64, 1)
         normed = (standard * gain).astype(BF16)
         both = mm(wt, normed, NT).astype(BF16).astype(F32)
         for p in range(2):
@@ -173,8 +187,17 @@
         own.start()
         own.wait()
 
+    turn[...] = jnp.swapaxes(w_ref[...].reshape(32, 32, 128).astype(F32), 0, 1)
+    for q in range(4):
+        for e2 in range(2):
+            at = q * 256 + e2 * 128
+            tile = turn[e2 * 16 + q * 4 : e2 * 16 + q * 4 + 4].reshape(128, 128)
+            wp_ref[at : at + 128] = tile.astype(BF16)
+            wpt_ref[:, at : at + 128] = tile.T.astype(BF16)
     for b in range(8):
         lt[:, b * 128 : (b + 1) * 128] = left[b * 128 : (b + 1) * 128].T[:64].astype(BF16)
+
+    bring.wait()
 
     def core_right(q):
         return copy_to(sr.at[1 - core, q], cr1.at[q], s1.at[q], r1.at[q], sibling)
@@ -308,6 +331,51 @@
                             pl.ds(pl.multiple_of(b * 1024 + i * 128, 128), 128),
                         ] = o[i * 32 : i * 32 + 32, e1 * 128 : e1 * 128 + 128]
 
+            @pl.when((q == 1) & (b == 0))
+            def _():
+                for d in range(1, 4):
+                    n = (x + d) % 4
+                    copy_to(cr2.at[n], cr2.at[n], s2.at[0], r2.at[n], sibling).wait_recv()
+                for d in (1, 2, 3, 0):
+                    zz = (z + d) % 4
+                    total = tr1[x, zz].astype(F32)
+                    for n in range(1, 4):
+                        total = total + cr2[(x + n) % 4, zz].astype(F32)
+                    tr2[zz] = total.astype(BF16)
+                    if d:
+                        z_right(d).start()
+
+            @pl.when((q == 2) & (b == 3))
+            def _():
+                for cp in lefts:
+                    cp.wait_recv()
+                cl[c] = glx[c]
+                total = cl[0].astype(F32)
+                for n in range(1, 8):
+                    total = total + cl[n].astype(F32)
+                tl[...] = total[:64].astype(BF16)
+                bias[...] = total[64:]
+                for d in range(1, 8):
+                    out_left(d).start()
+
+            @pl.when((q == 2) & (b == 2))
+            def _():
+                for d in range(1, 4):
+                    z_right(d).wait_recv()
+                total = tr2[z].astype(F32)
+                for n in range(1, 4):
+                    total = total + cr3[n].astype(F32)
+                tr3[...] = total.astype(BF16)
+                for cc in range(8):
+
+                    @unless((owner == r) & (c == cc))
+                    def _():
+                        out_right(cc).start()
+
+                @pl.when(owner == r)
+                def _():
+                    fr[piece] = tr3[...]
+
         gw = mm(ot[pl.ds(pl.multiple_of(q * 256, 256), 256)], g_ref[...])
         for cc in range(2):
             for zz in range(4):
@@ -319,51 +387,6 @@
         def _():
             pass_map(q - 1)
 
-        @pl.when(q == 1)
-        def _():
-            for d in range(1, 4):
-                n = (x + d) % 4
-                copy_to(cr2.at[n], cr2.at[n], s2.at[0], r2.at[n], sibling).wait_recv()
-            for d in (1, 2, 3, 0):
-                zz = (z + d) % 4
-                total = tr1[x, zz].astype(F32)
-                for n in range(1, 4):
-                    total = total + cr2[(x + n) % 4, zz].astype(F32)
-                tr2[zz] = total.astype(BF16)
-                if d:
-                    z_right(d).start()
-
-        @pl.when(q == 2)
-        def _():
-            for cp in lefts:
-                cp.wait_recv()
-            cl[c] = glx[c]
-            total = cl[0].astype(F32)
-            for n in range(1, 8):
-                total = total + cl[n].astype(F32)
-            tl[...] = total[:64].astype(BF16)
-            bias[...] = total[64:]
-            for d in range(1, 8):
-                out_left(d).start()
-
-        @pl.when(q == 3)
-        def _():
-            for d in range(1, 4):
-                z_right(d).wait_recv()
-            total = tr2[z].astype(F32)
-            for n in range(1, 4):
-                total = total + cr3[n].astype(F32)
-            tr3[...] = total.astype(BF16)
-            for cc in range(8):
-
-                @unless((owner == r) & (c == cc))
-                def _():
-                    out_right(cc).start()
-
-            @pl.when(owner == r)
-            def _():
-                fr[piece] = tr3[...]
-
     def z_map(d):
         zz = (z + d) % 4
         return copy_to(tw2.at[zz], cw3.at[d], s9.at[d], r9.at[d], (z_row(zz), c))
@@ -384,19 +407,20 @@
         def _():
             pass_map(3)
 
-        @pl.when(b == 3)
-        def _():
-            for d in range(1, 4):
-                n = (x + d) % 4
-                copy_to(cw2.at[n], cw2.at[n], s8.at[0], r8.at[n], sibling).wait_recv()
-            for d in (1, 2, 3, 0):
-                zz = (z + d) % 4
-                total = tw1[x, zz].astype(F32)
-                for n in range(1, 4):
-                    total = total + cw2[(x + n) % 4, zz].astype(F32)
-                tw2[zz] = total.astype(BF16)
-                if d:
-                    z_map(d).start()
+    put = pltpu.make_async_copy(pu_ref, pu_hbm, pu_sem)
+    put.start()
+
+    for d in range(1, 4):
+        n = (x + d) % 4
+        copy_to(cw2.at[n], cw2.at[n], s8.at[0], r8.at[n], sibling).wait_recv()
+    for d in (1, 2, 3, 0):
+        zz = (z + d) % 4
+        total = tw1[x, zz].astype(F32)
+        for n in range(1, 4):
+            total = total + cw2[(x + n) % 4, zz].astype(F32)
+        tw2[zz] = total.astype(BF16)
+        if d:
+            z_map(d).start()
 
     for d in range(1, 8):
         out_left(d).wait_recv()
@@ -407,6 +431,69 @@
         def _():
             copy_to(fr.at[n], fr.at[n], s4.at[n], r4.at[n], sibling).wait_recv()
 
+    closing[...] = jnp.swapaxes(fr[...].reshape(16, 32, 128).astype(F32), 0, 1)
+
+    def pair_grads(m):
+        even, odd = closing[2 * m], closing[2 * m + 1]
+        return jnp.concatenate(
+            [
+                fl[m // 2, pl.ds(pl.multiple_of((m % 2) * 32, 32), 32)],
+                jnp.where(low16, even, pltpu.roll(odd, 64, 1)).astype(BF16),
+                jnp.where(low16, pltpu.roll(even, 64, 1), odd).astype(BF16),
+            ],
+            axis=0,
+        )
+
+    acc[...] = jnp.zeros_like(acc)
+
+    @pl.loop(0, 16)
+    def _(m):
+        grads = pair_grads(m)
+        normed = (st[pl.ds(m * 2, 2)].reshape(128, 256) * gain).astype(BF16)
+        acc[...] += mm(grads, normed)
+        grads_all[m] = grads
+
+    for n in range(2):
+        for h in range(2):
+            at = h * 32
+            fs[n, at : at + 32] = acc[n * 32 : n * 32 + 32, h * 128 : h * 128 + 128]
+        fs[n, 64:80] = bias[...]
+    half = copy_to(fs.at[1 - core], fc1, s11.at[0], r11.at[0], sibling)
+    half.start()
+
+    def bring_adj(n):
+        return pltpu.make_async_copy(
+            adj_ref.at[n], adj_hbm.at[:, pl.ds(n * 8, 8)], adj_sem.at[n]
+        )
+
+    def adjoint(n):
+        @pl.loop(0, 4)
+        def _(p):
+            m = n * 4 + p
+            standard = st[pl.ds(m * 2, 2)].reshape(128, 256)
+            inverse = inv[pl.ds(m * 2, 2)].reshape(128, 1)
+            scaled = mm(grads_all[m], wt_ref[...], TN) * gain
+            mean = jnp.mean(scaled, -1, keepdims=True)
+            along = jnp.mean(scaled * standard, -1, keepdims=True)
+            adj = inverse * (scaled - mean - standard * along)
+            tall[pl.ds(p * 2, 2)] = adj.reshape(2, 64, 256)
+
+        @pl.loop(0, 8)
+        def _(b):
+            rows = pl.ds(pl.multiple_of(b * 8, 8), 8)
+            adj_ref[n, rows] = jnp.swapaxes(tall[:, rows], 0, 1)
+
+        bring_adj(n).start()
+
+    adjoint(0)
+    half.wait_recv()
+    fx[x] = (fs[core] + fc1[...]).astype(BF16)
+    fxs = [
+        copy_to(fx.at[x], fx.at[x], s13.at[d], r13.at[d], (x_row((x + d) % 4), c)) for d in range(1, 4)
+    ]
+    for cp in fxs:
+        cp.start()
+    adjoint(1)
     for d in range(1, 4):
         z_map(d).wait_recv()
     total = tw2[z].astype(F32)
@@ -415,38 +502,28 @@
     cw4[c] = total.astype(BF16)
     for d in range(1, 8):
         col_map(d).start()
-
-    closing[...] = jnp.swapaxes(fr[...].reshape(16, 32, 128).astype(F32), 0, 1)
-    acc[...] = jnp.zeros_like(acc)
-
-    @pl.loop(0, 16)
-    def _(m):
-        xs = x_ref[pl.ds(m * 2, 2)].astype(F32).reshape(128, 256)
-        standard, inverse = normalise(xs)
-        normed = (standard * gain).astype(BF16)
-        even, odd = closing[2 * m], closing[2 * m + 1]
-        grads = jnp.concatenate(
-            [
-                fl[m // 2, pl.ds(pl.multiple_of((m % 2) * 32, 32), 32)],
-                jnp.where(low16, even, pltpu.roll(odd, 64, 1)).astype(BF16),
-                jnp.where(low16, pltpu.roll(even, 64, 1), odd).astype(BF16),
-            ],
-            axis=0,
-        )
-        acc[...] += mm(grads, normed)
-        scaled = mm(grads, wt, TN) * gain
-        mean = jnp.mean(scaled, -1, keepdims=True)
-        along = jnp.mean(scaled * standard, -1, keepdims=True)
-        adj = inverse * (scaled - mean - standard * along)
-        adj_ref[pl.ds(m * 2, 2)] = adj.reshape(2, 64, 256)
-
-    for n in range(2):
-        for h in range(2):
-            at = h * 32
-            fs[n, at : at + 32] = acc[n * 32 : n * 32 + 32, h * 128 : h * 128 + 128]
-        fs[n, 64:80] = bias[...]
-    half = copy_to(fs.at[1 - core], fc1, s11.at[0], r11.at[0], sibling)
-    half.start()
+    adjoint(2)
+    for cp in fxs:
+        cp.wait_recv()
+    total = fx[0].astype(F32)
+    for n in range(1, 4):
+        total = total + fx[n].astype(F32)
+    fz[z] = total.astype(BF16)
+    fzs = [
+        copy_to(fz.at[z], fz.at[z], s15.at[d], r15.at[d], (z_row((z + d) % 4), c)) for d in range(1, 4)
+    ]
+    for cp in fzs:
+        cp.start()
+    adjoint(3)
+    for cp in fzs:
+        cp.wait_recv()
+    total = fz[0].astype(F32)
+    for n in range(1, 4):
+        total = total + fz[n].astype(F32)
+    ff[core] = total[:64]
+    end = copy_to(ff.at[core], ff.at[core], s11.at[1], r11.at[1], sibling)
+    end.start()
+    bias_ref[...] = jnp.sum(total[64:], 0, keepdims=True)
     for d in range(1, 8):
         col_map(d).wait_recv()
     total = cw4[0].astype(F32)
@@ -458,13 +535,10 @@
     ]
     for cp in zs:
         cp.start()
-    half.wait_recv()
-    fx[x] = (fs[core] + fc1[...]).astype(BF16)
-    fxs = [
-        copy_to(fx.at[x], fx.at[x], s13.at[d], r13.at[d], (x_row((x + d) % 4), c)) for d in range(1, 4)
-    ]
-    for cp in fxs:
-        cp.start()
+    end.wait_recv()
+    for n in range(2):
+        for h in range(2):
+            fac_ref[n, :, h * 128 : h * 128 + 128] = ff[n, h * 32 : h * 32 + 32]
     for cp in zs:
         cp.wait_recv()
     wx[x] = wz[...]
@@ -473,35 +547,19 @@
     ]
     for cp in xs_:
         cp.start()
-    for cp in fxs:
-        cp.wait_recv()
-    total = fx[0].astype(F32)
-    for n in range(1, 4):
-        total = total + fx[n].astype(F32)
-    fz[z] = total.astype(BF16)
-    fzs = [
-        copy_to(fz.at[z], fz.at[z], s15.at[d], r15.at[d], (z_row((z + d) % 4), c)) for d in range(1, 4)
-    ]
-    for cp in fzs:
-        cp.start()
     for cp in xs_:
         cp.wait_recv()
     last = copy_to(wx, wc, s16.at[0], r16.at[0], sibling)
     last.start()
-    map_ref[core] = wx[...]
-    for cp in fzs:
-        cp.wait_recv()
-    total = fz[0].astype(F32)
-    for n in range(1, 4):
-        total = total + fz[n].astype(F32)
-    ff[core] = total[:64]
-    end = copy_to(ff.at[core], ff.at[core], s11.at[1], r11.at[1], sibling)
-    end.start()
-    bias_ref[...] = total[64:]
+
+    def spread(e2, parts):
+        map_ref[:, pl.ds(pl.multiple_of(e2 * 16, 16), 16)] = jnp.swapaxes(
+            parts.reshape(16, 32, 128).astype(F32), 0, 1
+        )
+
+    spread(core, wx[...])
     last.wait_recv()
-    map_ref[1 - core] = wc[...]
-    end.wait_recv()
-    fac_ref[...] = ff[...]
+    spread(1 - core, wc[...])
 
     for step in range(16):
         sends, cp = give(step)
@@ -533,12 +591,16 @@
         def _():
             out_right(cc).wait_send()
 
+    put.wait()
+    for n in range(4):
+        bring_adj(n).wait()
     for cp in lefts + zs + fxs + xs_ + fzs + [half, last, end]:
         cp.wait_send()
 
 
-def run(x, gain, wt, g, wp, wpt, off):
+def run(x, gain, w1, w2, g, w, off):
     vm = pl.BlockSpec(memory_space=pltpu.VMEM)
+    anywhere = pl.BlockSpec(memory_space=pl.ANY)
 
     def b16(*shape):
         return pltpu.VMEM(shape, BF16)
@@ -553,14 +615,16 @@
         kernel,
         out_shape=(
             jax.ShapeDtypeStruct((4096, 128), BF16),
-            jax.ShapeDtypeStruct((32, 64, 256), F32),
-            jax.ShapeDtypeStruct((2, 64, 128), F32),
-            jax.ShapeDtypeStruct((16, 128), F32),
-            jax.ShapeDtypeStruct((2, 4, 4, 32, 128), BF16),
+            jax.ShapeDtypeStruct((64, 32, 256), F32),
+            jax.ShapeDtypeStruct((2, 32, 256), F32),
+            jax.ShapeDtypeStruct((1, 128), F32),
+            jax.ShapeDtypeStruct((32, 32, 128), F32),
         ),
-        in_specs=[vm] * 7,
-        out_specs=(vm,) * 5,
+        in_specs=[vm, vm, vm, vm, anywhere, vm, vm],
+        out_specs=(anywhere, anywhere, vm, vm, vm),
         scratch_shapes=[
+            f32(32, 64, 256), f32(32, 64, 1), b16(4096, 128), b16(64, 256), b16(1024, 128), b16(128, 1024),
+            b16(4096, 128), f32(32, 32, 128), f32(4, 64, 8, 256),
             b16(1024, 128), b16(1024, 128), b16(64, 1024), f32(1024, 128), f32(32, 16, 128),
             b16(16, 32, 128), b16(16, 4, 32, 128), b16(1024, 4096), b16(1024, 4096), b16(8, 80, 128),
             b16(2, 4, 4, 64, 128), b16(4, 4, 64, 128), b16(4, 4, 64, 128), b16(4, 4, 64, 128),
@@ -569,16 +633,17 @@
             b16(4, 32, 128), b16(4, 32, 128), b16(8, 32, 128), b16(4, 32, 128), b16(4, 4, 32, 128),
             b16(4, 4, 32, 128),
             b16(8, 80, 128), b16(64, 128), b16(8, 64, 128), f32(16, 128), f32(32, 16, 128), f32(64, 256),
-            f32(2, 80, 128), f32(80, 128), b16(4, 80, 128), b16(4, 80, 128), f32(2, 64, 128),
+            b16(16, 64, 128), f32(8, 64, 256), f32(2, 80, 128), f32(80, 128), b16(4, 80, 128), b16(4, 80, 128), f32(2, 64, 128),
             pltpu.SemaphoreType.DMA((16,)), pltpu.SemaphoreType.DMA((8,)),
             pltpu.SemaphoreType.DMA((8,)), pltpu.SemaphoreType.DMA((8,)), pltpu.SemaphoreType.DMA,
+            pltpu.SemaphoreType.DMA, pltpu.SemaphoreType.DMA, pltpu.SemaphoreType.DMA((4,)),
             *sems,
         ],
         compiler_params=pltpu.CompilerParams(
             collective_id=0, has_side_effects=True, vmem_limit_bytes=56 << 20
         ),
         name="outer_product_mean",
-    )(x, gain, wt, g, wp, wpt, off)
+    )(x, gain, w1, w2, g, w, off)
 
 
 def per_device(
@@ -590,25 +655,21 @@
     emitted_offset,
     upstream_adjoint,
 ):
-    x = sequence_stack.transpose(1, 0, 2)
-    wt = jnp.concatenate([first_factor_map.T, second_factor_map.T], axis=0)
-    wp = emitted_map.reshape(32, 2, 4, 4, 128).transpose(2, 1, 3, 0, 4).reshape(1024, 128)
     pu, adj, fac, bias, w = run(
-        x,
+        sequence_stack,
         feature_multiplier.reshape(1, 256),
-        wt,
+        first_factor_map.T,
+        second_factor_map.T,
         upstream_adjoint.reshape(4096, 128),
-        wp,
-        wp.T,
+        emitted_map,
         emitted_offset.reshape(1, 128),
     )
-    factor = fac.reshape(2, 2, 32, 128).transpose(0, 2, 1, 3).reshape(2, 32, 256).transpose(0, 2, 1)
     return (
         pu.reshape(32, 128, 128),
-        adj.transpose(1, 0, 2),
-        factor,
-        w.reshape(32, 32, 128).transpose(1, 0, 2).reshape(1024, 128).astype(F32),
-        jnp.sum(bias, 0),
+        adj,
+        fac.transpose(0, 2, 1),
+        w.reshape(1024, 128),
+        bias.reshape(128),
     )
 
 

time: 82.9 us -> 77.5 us (0.935)
  local copies, waits for them, and re-layouts: 11.6 us -> 5.73 us
  other arithmetic: 1.94 us -> 0 us
  Pallas kernels: 68.2 us -> 70.1 us
    unnamed x13, local copies, waits for them, and re-layouts: 8 us -> 5.73 us
    pallas_call x1, Pallas kernels: 68.2 us -> 70.1 us  [run(): pl.pallas_call(kernel, out_shape=(jax.ShapeDtypeStruct((4096, 128), BF16)...]
    reshape x2 -> x0, local copies, waits for them, and re-layouts: 1.48 us -> none  [the longest x1 0.85 us: per_device(): emitted_map.reshape(32, 2, 4, 4, 128).transpose(2, 1, 3, 0, 4)]
    concatenate x1 -> x0, other arithmetic: 1.35 us -> none  [per_device(): wt = jnp.concatenate([first_factor_map.T, second_factor_map.T], axis=0)]
    convert_element_type x1 -> x0, local copies, waits for them, and re-layouts: 1.1 us -> none  [per_device(): w.reshape(32, 32, 128).transpose(1, 0, 2).reshape(1024, 128).astype(F32)]
    transpose x1 -> x0, local copies, waits for them, and re-layouts: 1.05 us -> none  [per_device(): emitted_map.reshape(32, 2, 4, 4, 128).transpose(2, 1, 3, 0, 4)]
where the time goes in v3:
time: 77.5 us; the launch traced here: 76.5 us
  Pallas kernels  70.1 us (90%)
  local copies, waits for them, and re-layouts  5.73 us (7%)
    pallas_call x1, Pallas kernels, run(): pl.pallas_call(kernel, out_shape=(jax.ShapeDtypeStruct((4096, 128), BF16)...  70.1 us
    unnamed x13, local copies, waits for them, and re-layouts  5.73 us

profile of v3, /device:TPU:1, one launch (start us, length us, event | category | flops | bytes accessed | tf_op | source)
XLA Modules:
  0.0 76.5 jit_solution(9863021667912651020)
XLA Ops:
  0.6 70.1 %outer_product_mean.1 = (bf16[4096,128]{1,0:T(8,128)(2,1)}, f32[64,32,256]{2,1,0:T(8,128)}, f32[2,32,256]{2,1,0:T(8,128)}, f32[1,128]{1,0:T(1,128)}, f32[32,32,128]{2,1,0:T(8,128)}) custom-call(bf16[64,32,256]{2,1,0:T(8,128)(2,1)} %x_ref.1, f32[1,256]{1,0:T(1,128)} %bitcast.15, bf16[32,256]{1,0:T(8,128)(2,1)} %bitcast.13, bf16[32,256]{1,0:T(8,128)(2,1)} %bitcast.14, ...), custom_call_target="tpu_custom_call" | custom-call | tf_op jit(solution)/shard_map/outer_product_mean/pallas_call | solution.py:614
  70.8 0.0 copy-start
  70.8 2.5 %copy.17 = bf16[32,128,128]{2,1,0:T(8,128)(2,1)} copy(bf16[32,128,128]{2,1,0:T(8,128)(2,1)} %bitcast.10) | data formatting | bytes 2097152
  73.2 0.0 copy-done
  73.2 0.0 copy-start.2
  73.2 0.0 copy-start.1
  73.2 0.0 copy-start.3
  73.3 1.3 %copy.18 = f32[64,32,256]{2,1,0:T(8,128)} copy(f32[64,32,256]{2,1,0:T(8,128)S(1)} %copy-done) | data formatting | bytes 4194304
  74.6 0.0 copy-done.2
  74.6 0.6 copy.19
  75.2 0.0 copy-done.1
  75.2 0.8 %copy.20 = f32[1024,128]{1,0:T(8,128)} copy(f32[1024,128]{1,0:T(8,128)S(1)} %bitcast.11) | data formatting | bytes 1048576
  76.0 0.0 copy-done.3
  76.0 0.5 copy.21
Async XLA Ops:
  70.8 2.5 %copy-start = (f32[64,32,256]{2,1,0:T(8,128)S(1)}, f32[64,32,256]{2,1,0:T(8,128)}, u32[]{:S(2)}) copy-start(f32[64,32,256]{2,1,0:T(8,128)} %get-tuple-element.21) | copy-start | bytes 6291460
  73.2 1.3 %copy-start.2 = (f32[2,32,256]{2,1,0:T(8,128)S(1)}, f32[2,32,256]{2,1,0:T(8,128)}, u32[]{:S(2)}) copy-start(f32[2,32,256]{2,1,0:T(8,128)} %get-tuple-element.12) | copy-start | bytes 196612
  73.2 2.0 %copy-start.1 = (f32[32,32,128]{2,1,0:T(8,128)S(1)}, f32[32,32,128]{2,1,0:T(8,128)}, u32[]{:S(2)}) copy-start(f32[32,32,128]{2,1,0:T(8,128)} %get-tuple-element.13) | copy-start | bytes 1572868
  73.2 2.8 %copy-start.3 = (f32[1,128]{1,0:T(1,128)S(1)}, f32[1,128]{1,0:T(1,128)}, u32[]{:S(2)}) copy-start(f32[1,128]{1,0:T(1,128)} %get-tuple-element.14) | copy-start | bytes 1540

commit v4 on v3

--- a/solution.py
+++ b/solution.py
@@ -217,14 +217,14 @@
     def _(q):
         wq = wp_ref[pl.ds(pl.multiple_of(q * 256, 256), 256)]
 
-        @pl.loop(0, 4)
+        @pl.loop(0, 2)
         def _(b):
-            g = g_ref[pl.ds(pl.multiple_of(b * 1024, 1024), 1024)]
+            g = g_ref[pl.ds(pl.multiple_of(b * 2048, 2048), 2048)]
             d = mm(wq, g, NT).astype(BF16)
             for e in range(8):
-                for i in range(8):
+                for i in range(16):
                     dt[
-                        pl.ds(pl.multiple_of(b * 256 + i * 32, 32), 32),
+                        pl.ds(pl.multiple_of(b * 512 + i * 32, 32), 32),
                         pl.ds(pl.multiple_of(q * 1024 + e * 128, 128), 128),
                     ] = d[e * 32 : e * 32 + 32, i * 128 : i * 128 + 128]
 
@@ -319,19 +319,19 @@
     def _(q):
         part = land[pl.ds(q * 4, 4)].reshape(512, 128)
 
-        @pl.loop(0, 4)
+        @pl.loop(0, 2)
         def _(b):
-            rows = pl.ds(pl.multiple_of(b * 256, 256), 256)
+            rows = pl.ds(pl.multiple_of(b * 512, 512), 512)
             for e2, l in enumerate((la, lb)):
                 o = mm(l[rows], part, NT).astype(BF16)
                 for e1 in range(4):
-                    for i in range(8):
+                    for i in range(16):
                         ot[
                             pl.ds(pl.multiple_of(q * 256 + (e2 * 4 + e1) * 32, 32), 32),
-                            pl.ds(pl.multiple_of(b * 1024 + i * 128, 128), 128),
+                            pl.ds(pl.multiple_of(b * 2048 + i * 128, 128), 128),
                         ] = o[i * 32 : i * 32 + 32, e1 * 128 : e1 * 128 + 128]
 
-            @pl.when((q == 1) & (b == 0))
+            @pl.when((q == 0) & (b == 1))
             def _():
                 for d in range(1, 4):
                     n = (x + d) % 4
@@ -345,7 +345,7 @@
                     if d:
                         z_right(d).start()
 
-            @pl.when((q == 2) & (b == 3))
+            @pl.when((q == 2) & (b == 1))
             def _():
                 for cp in lefts:
                     cp.wait_recv()
@@ -358,7 +358,7 @@
                 for d in range(1, 8):
                     out_left(d).start()
 
-            @pl.when((q == 2) & (b == 2))
+            @pl.when((q == 1) & (b == 1))
             def _():
                 for d in range(1, 4):
                     z_right(d).wait_recv()
@@ -425,6 +425,14 @@
     for d in range(1, 8):
         out_left(d).wait_recv()
     fl[c] = tl[...]
+    for d in range(1, 4):
+        z_map(d).wait_recv()
+    total = tw2[z].astype(F32)
+    for n in range(1, 4):
+        total = total + cw3[n].astype(F32)
+    cw4[c] = total.astype(BF16)
+    for d in range(1, 8):
+        col_map(d).start()
     for n in range(8):
 
         @unless((source(n) == r) & (goal == c))
@@ -494,15 +502,18 @@
     for cp in fxs:
         cp.start()
     adjoint(1)
-    for d in range(1, 4):
-        z_map(d).wait_recv()
-    total = tw2[z].astype(F32)
-    for n in range(1, 4):
-        total = total + cw3[n].astype(F32)
-    cw4[c] = total.astype(BF16)
+    adjoint(2)
     for d in range(1, 8):
-        col_map(d).start()
-    adjoint(2)
+        col_map(d).wait_recv()
+    total = cw4[0].astype(F32)
+    for n in range(1, 8):
+        total = total + cw4[n].astype(F32)
+    wz[z] = total.astype(BF16)
+    zs = [
+        copy_to(wz.at[z], wz.at[z], s12.at[d], r12.at[d], (z_row((z + d) % 4), c)) for d in range(1, 4)
+    ]
+    for cp in zs:
+        cp.start()
     for cp in fxs:
         cp.wait_recv()
     total = fx[0].astype(F32)
@@ -515,6 +526,14 @@
     for cp in fzs:
         cp.start()
     adjoint(3)
+    for cp in zs:
+        cp.wait_recv()
+    wx[x] = wz[...]
+    xs_ = [
+        copy_to(wx.at[x], wx.at[x], s14.at[d], r14.at[d], (x_row((x + d) % 4), c)) for d in range(1, 4)
+    ]
+    for cp in xs_:
+        cp.start()
     for cp in fzs:
         cp.wait_recv()
     total = fz[0].astype(F32)
@@ -524,29 +543,10 @@
     end = copy_to(ff.at[core], ff.at[core], s11.at[1], r11.at[1], sibling)
     end.start()
     bias_ref[...] = jnp.sum(total[64:], 0, keepdims=True)
-    for d in range(1, 8):
-        col_map(d).wait_recv()
-    total = cw4[0].astype(F32)
-    for n in range(1, 8):
-        total = total + cw4[n].astype(F32)
-    wz[z] = total.astype(BF16)
-    zs = [
-        copy_to(wz.at[z], wz.at[z], s12.at[d], r12.at[d], (z_row((z + d) % 4), c)) for d in range(1, 4)
-    ]
-    for cp in zs:
-        cp.start()
     end.wait_recv()
     for n in range(2):
         for h in range(2):
             fac_ref[n, :, h * 128 : h * 128 + 128] = ff[n, h * 32 : h * 32 + 32]
-    for cp in zs:
-        cp.wait_recv()
-    wx[x] = wz[...]
-    xs_ = [
-        copy_to(wx.at[x], wx.at[x], s14.at[d], r14.at[d], (x_row((x + d) % 4), c)) for d in range(1, 4)
-    ]
-    for cp in xs_:
-        cp.start()
     for cp in xs_:
         cp.wait_recv()
     last = copy_to(wx, wc, s16.at[0], r16.at[0], sibling)

time: 77.5 us -> 72.5 us (0.935); the launches traced: 76.5 us -> 72.3 us
  Pallas kernels: 70.1 us -> 65.9 us
    pallas_call x1, Pallas kernels: 70.1 us -> 65.9 us  [run(): pl.pallas_call(kernel, out_shape=(jax.ShapeDtypeStruct((4096, 128), BF16)...]
where the time goes in v4:
time: 72.5 us; the launch traced here: 72.3 us
  Pallas kernels  65.9 us (91%)
  local copies, waits for them, and re-layouts  5.73 us (8%)
    pallas_call x1, Pallas kernels, run(): pl.pallas_call(kernel, out_shape=(jax.ShapeDtypeStruct((4096, 128), BF16)...  65.9 us
    unnamed x13, local copies, waits for them, and re-layouts  5.73 us

profile of v4, /device:TPU:1, one launch (start us, length us, event | category | flops | bytes accessed | tf_op | source)
XLA Modules:
  0.0 72.3 jit_solution(15216959285176800342)
XLA Ops:
  0.6 65.9 %outer_product_mean.1 = (bf16[4096,128]{1,0:T(8,128)(2,1)}, f32[64,32,256]{2,1,0:T(8,128)}, f32[2,32,256]{2,1,0:T(8,128)}, f32[1,128]{1,0:T(1,128)}, f32[32,32,128]{2,1,0:T(8,128)}) custom-call(bf16[64,32,256]{2,1,0:T(8,128)(2,1)} %x_ref.1, f32[1,256]{1,0:T(1,128)} %bitcast.15, bf16[32,256]{1,0:T(8,128)(2,1)} %bitcast.13, bf16[32,256]{1,0:T(8,128)(2,1)} %bitcast.14, ...), custom_call_target="tpu_custom_call" | custom-call | tf_op jit(solution)/shard_map/outer_product_mean/pallas_call | solution.py:614
  66.6 0.0 copy-start
  66.6 2.5 %copy.17 = bf16[32,128,128]{2,1,0:T(8,128)(2,1)} copy(bf16[32,128,128]{2,1,0:T(8,128)(2,1)} %bitcast.10) | data formatting | bytes 2097152
  69.0 0.0 copy-done
  69.0 0.0 copy-start.2
  69.0 0.0 copy-start.1
  69.0 0.0 copy-start.3
  69.1 1.3 %copy.18 = f32[64,32,256]{2,1,0:T(8,128)} copy(f32[64,32,256]{2,1,0:T(8,128)S(1)} %copy-done) | data formatting | bytes 4194304
  70.4 0.0 copy-done.2
  70.4 0.6 copy.19
  71.0 0.0 copy-done.1
  71.0 0.8 %copy.20 = f32[1024,128]{1,0:T(8,128)} copy(f32[1024,128]{1,0:T(8,128)S(1)} %bitcast.11) | data formatting | bytes 1048576
  71.8 0.0 copy-done.3
  71.8 0.5 copy.21
Async XLA Ops:
  66.6 2.5 %copy-start = (f32[64,32,256]{2,1,0:T(8,128)S(1)}, f32[64,32,256]{2,1,0:T(8,128)}, u32[]{:S(2)}) copy-start(f32[64,32,256]{2,1,0:T(8,128)} %get-tuple-element.21) | copy-start | bytes 6291460
  69.0 1.3 %copy-start.2 = (f32[2,32,256]{2,1,0:T(8,128)S(1)}, f32[2,32,256]{2,1,0:T(8,128)}, u32[]{:S(2)}) copy-start(f32[2,32,256]{2,1,0:T(8,128)} %get-tuple-element.12) | copy-start | bytes 196612
  69.0 2.0 %copy-start.1 = (f32[32,32,128]{2,1,0:T(8,128)S(1)}, f32[32,32,128]{2,1,0:T(8,128)}, u32[]{:S(2)}) copy-start(f32[32,32,128]{2,1,0:T(8,128)} %get-tuple-element.13) | copy-start | bytes 1572868
  69.0 2.8 %copy-start.3 = (f32[1,128]{1,0:T(1,128)S(1)}, f32[1,128]{1,0:T(1,128)}, u32[]{:S(2)}) copy-start(f32[1,128]{1,0:T(1,128)} %get-tuple-element.14) | copy-start | bytes 1540

commit v5 on v4

--- a/solution.py
+++ b/solution.py
@@ -123,7 +123,7 @@
     wt = jnp.concatenate([w1_ref[...], w2_ref[...]], axis=0)
     wt_ref[...] = wt
 
-    @pl.loop(0, 8)
+    @pl.loop(0, 8, unroll=4)
     def _(b):
         rows = pl.ds(pl.multiple_of(b * 8, 8), 8)
         for h in range(2):
@@ -133,7 +133,7 @@
     low32 = low_lanes((32, 128))
     low16 = low_lanes((16, 128))
 
-    @pl.loop(0, 8)
+    @pl.loop(0, 8, unroll=2)
     def _(b):
         standard, inverse = normalise(st[pl.ds(b * 4, 4)].reshape(256, 256))
         st[pl.ds(b * 4, 4)] = standard.reshape(4, 64, 256)
@@ -217,7 +217,7 @@
     def _(q):
         wq = wp_ref[pl.ds(pl.multiple_of(q * 256, 256), 256)]
 
-        @pl.loop(0, 2)
+        @pl.loop(0, 2, unroll=2)
         def _(b):
             g = g_ref[pl.ds(pl.multiple_of(b * 2048, 2048), 2048)]
             d = mm(wq, g, NT).astype(BF16)
@@ -265,7 +265,7 @@
 
     bias[...] = jnp.zeros_like(bias)
 
-    @pl.loop(0, 4)
+    @pl.loop(0, 4, unroll=2)
     def _(b):
         rows = pl.ds(pl.multiple_of(b * 256, 256), 256)
         first = jnp.zeros((256, 128), F32)
@@ -319,7 +319,7 @@
     def _(q):
         part = land[pl.ds(q * 4, 4)].reshape(512, 128)
 
-        @pl.loop(0, 2)
+        @pl.loop(0, 2, unroll=2)
         def _(b):
             rows = pl.ds(pl.multiple_of(b * 512, 512), 512)
             for e2, l in enumerate((la, lb)):
@@ -331,50 +331,50 @@
                             pl.ds(pl.multiple_of(b * 2048 + i * 128, 128), 128),
                         ] = o[i * 32 : i * 32 + 32, e1 * 128 : e1 * 128 + 128]
 
-            @pl.when((q == 0) & (b == 1))
+        @pl.when(q == 0)
+        def _():
+            for d in range(1, 4):
+                n = (x + d) % 4
+                copy_to(cr2.at[n], cr2.at[n], s2.at[0], r2.at[n], sibling).wait_recv()
+            for d in (1, 2, 3, 0):
+                zz = (z + d) % 4
+                total = tr1[x, zz].astype(F32)
+                for n in range(1, 4):
+                    total = total + cr2[(x + n) % 4, zz].astype(F32)
+                tr2[zz] = total.astype(BF16)
+                if d:
+                    z_right(d).start()
+
+        @pl.when(q == 2)
+        def _():
+            for cp in lefts:
+                cp.wait_recv()
+            cl[c] = glx[c]
+            total = cl[0].astype(F32)
+            for n in range(1, 8):
+                total = total + cl[n].astype(F32)
+            tl[...] = total[:64].astype(BF16)
+            bias[...] = total[64:]
+            for d in range(1, 8):
+                out_left(d).start()
+
+        @pl.when(q == 1)
+        def _():
+            for d in range(1, 4):
+                z_right(d).wait_recv()
+            total = tr2[z].astype(F32)
+            for n in range(1, 4):
+                total = total + cr3[n].astype(F32)
+            tr3[...] = total.astype(BF16)
+            for cc in range(8):
+
+                @unless((owner == r) & (c == cc))
+                def _():
+                    out_right(cc).start()
+
+            @pl.when(owner == r)
             def _():
-                for d in range(1, 4):
-                    n = (x + d) % 4
-                    copy_to(cr2.at[n], cr2.at[n], s2.at[0], r2.at[n], sibling).wait_recv()
-                for d in (1, 2, 3, 0):
-                    zz = (z + d) % 4
-                    total = tr1[x, zz].astype(F32)
-                    for n in range(1, 4):
-                        total = total + cr2[(x + n) % 4, zz].astype(F32)
-                    tr2[zz] = total.astype(BF16)
-                    if d:
-                        z_right(d).start()
-
-            @pl.when((q == 2) & (b == 1))
-            def _():
-                for cp in lefts:
-                    cp.wait_recv()
-                cl[c] = glx[c]
-                total = cl[0].astype(F32)
-                for n in range(1, 8):
-                    total = total + cl[n].astype(F32)
-                tl[...] = total[:64].astype(BF16)
-                bias[...] = total[64:]
-                for d in range(1, 8):
-                    out_left(d).start()
-
-            @pl.when((q == 1) & (b == 1))
-            def _():
-                for d in range(1, 4):
-                    z_right(d).wait_recv()
-                total = tr2[z].astype(F32)
-                for n in range(1, 4):
-                    total = total + cr3[n].astype(F32)
-                tr3[...] = total.astype(BF16)
-                for cc in range(8):
-
-                    @unless((owner == r) & (c == cc))
-                    def _():
-                        out_right(cc).start()
-
-                @pl.when(owner == r)
-                def _():
-                    fr[piece] = tr3[...]
+                fr[piece] = tr3[...]
 
         gw = mm(ot[pl.ds(pl.multiple_of(q * 256, 256), 256)], g_ref[...])
         for cc in range(2):
@@ -454,7 +454,7 @@
 
     acc[...] = jnp.zeros_like(acc)
 
-    @pl.loop(0, 16)
+    @pl.loop(0, 16, unroll=4)
     def _(m):
         grads = pair_grads(m)
         normed = (st[pl.ds(m * 2, 2)].reshape(128, 256) * gain).astype(BF16)
@@ -475,7 +475,7 @@
         )
 
     def adjoint(n):
-        @pl.loop(0, 4)
+        @pl.loop(0, 4, unroll=2)
         def _(p):
             m = n * 4 + p
             standard = st[pl.ds(m * 2, 2)].reshape(128, 256)
@@ -486,7 +486,7 @@
             adj = inverse * (scaled - mean - standard * along)
             tall[pl.ds(p * 2, 2)] = adj.reshape(2, 64, 256)
 
-        @pl.loop(0, 8)
+        @pl.loop(0, 8, unroll=4)
         def _(b):
             rows = pl.ds(pl.multiple_of(b * 8, 8), 8)
             adj_ref[n, rows] = jnp.swapaxes(tall[:, rows], 0, 1)

time: 72.5 us -> 71.4 us (0.985)
  Pallas kernels: 65.9 us -> 64.9 us
    pallas_call x1, Pallas kernels: 65.9 us -> 64.9 us  [run(): pl.pallas_call(kernel, out_shape=(jax.ShapeDtypeStruct((4096, 128), BF16)...]
where the time goes in v5:
time: 71.4 us; the launch traced here: 71.3 us
  Pallas kernels  64.9 us (91%)
  local copies, waits for them, and re-layouts  5.73 us (8%)
    pallas_call x1, Pallas kernels, run(): pl.pallas_call(kernel, out_shape=(jax.ShapeDtypeStruct((4096, 128), BF16)...  64.9 us
    unnamed x13, local copies, waits for them, and re-layouts  5.73 us

profile of v5, /device:TPU:1, one launch (start us, length us, event | category | flops | bytes accessed | tf_op | source)
XLA Modules:
  0.0 71.3 jit_solution(13674808972949384106)
XLA Ops:
  0.6 64.9 %outer_product_mean.1 = (bf16[4096,128]{1,0:T(8,128)(2,1)}, f32[64,32,256]{2,1,0:T(8,128)}, f32[2,32,256]{2,1,0:T(8,128)}, f32[1,128]{1,0:T(1,128)}, f32[32,32,128]{2,1,0:T(8,128)}) custom-call(bf16[64,32,256]{2,1,0:T(8,128)(2,1)} %x_ref.1, f32[1,256]{1,0:T(1,128)} %bitcast.15, bf16[32,256]{1,0:T(8,128)(2,1)} %bitcast.13, bf16[32,256]{1,0:T(8,128)(2,1)} %bitcast.14, ...), custom_call_target="tpu_custom_call" | custom-call | tf_op jit(solution)/shard_map/outer_product_mean/pallas_call | solution.py:614
  65.5 0.0 copy-start
  65.5 2.5 %copy.17 = bf16[32,128,128]{2,1,0:T(8,128)(2,1)} copy(bf16[32,128,128]{2,1,0:T(8,128)(2,1)} %bitcast.10) | data formatting | bytes 2097152
  68.0 0.0 copy-done
  68.0 0.0 copy-start.2
  68.0 0.0 copy-start.1
  68.0 0.0 copy-start.3
  68.0 1.3 %copy.18 = f32[64,32,256]{2,1,0:T(8,128)} copy(f32[64,32,256]{2,1,0:T(8,128)S(1)} %copy-done) | data formatting | bytes 4194304
  69.3 0.0 copy-done.2
  69.3 0.6 copy.19
  70.0 0.0 copy-done.1
  70.0 0.8 %copy.20 = f32[1024,128]{1,0:T(8,128)} copy(f32[1024,128]{1,0:T(8,128)S(1)} %bitcast.11) | data formatting | bytes 1048576
  70.7 0.0 copy-done.3
  70.8 0.5 copy.21
Async XLA Ops:
  65.5 2.5 %copy-start = (f32[64,32,256]{2,1,0:T(8,128)S(1)}, f32[64,32,256]{2,1,0:T(8,128)}, u32[]{:S(2)}) copy-start(f32[64,32,256]{2,1,0:T(8,128)} %get-tuple-element.21) | copy-start | bytes 6291460
  68.0 1.3 %copy-start.2 = (f32[2,32,256]{2,1,0:T(8,128)S(1)}, f32[2,32,256]{2,1,0:T(8,128)}, u32[]{:S(2)}) copy-start(f32[2,32,256]{2,1,0:T(8,128)} %get-tuple-element.12) | copy-start | bytes 196612
  68.0 2.0 %copy-start.1 = (f32[32,32,128]{2,1,0:T(8,128)S(1)}, f32[32,32,128]{2,1,0:T(8,128)}, u32[]{:S(2)}) copy-start(f32[32,32,128]{2,1,0:T(8,128)} %get-tuple-element.13) | copy-start | bytes 1572868
  68.0 2.8 %copy-start.3 = (f32[1,128]{1,0:T(1,128)S(1)}, f32[1,128]{1,0:T(1,128)}, u32[]{:S(2)}) copy-start(f32[1,128]{1,0:T(1,128)} %get-tuple-element.14) | copy-start | bytes 1540

commit v6 on v5

--- a/solution.py
+++ b/solution.py
@@ -331,7 +331,7 @@
                             pl.ds(pl.multiple_of(b * 2048 + i * 128, 128), 128),
                         ] = o[i * 32 : i * 32 + 32, e1 * 128 : e1 * 128 + 128]
 
-        @pl.when(q == 0)
+        @pl.when(q == 1)
         def _():
             for d in range(1, 4):
                 n = (x + d) % 4
@@ -345,7 +345,7 @@
                 if d:
                     z_right(d).start()
 
-        @pl.when(q == 2)
+        @pl.when(q == 3)
         def _():
             for cp in lefts:
                 cp.wait_recv()
@@ -358,7 +358,7 @@
             for d in range(1, 8):
                 out_left(d).start()
 
-        @pl.when(q == 1)
+        @pl.when(q == 2)
         def _():
             for d in range(1, 4):
                 z_right(d).wait_recv()
@@ -646,6 +646,34 @@
     )(x, gain, w1, w2, g, w, off)
 
 
+def hand_over_kernel(*refs):
+    sources, goals, sem = refs[:5], refs[5:10], refs[10]
+    copies = []
+    for source, goal, parts in zip(sources, goals, (4, 8, 1, 1, 1)):
+        rows = source.shape[0] // parts
+        for n in range(parts):
+            at = pl.ds(n * rows, rows)
+            copies.append((source.at[at], goal.at[at]))
+    copies = [pltpu.make_async_copy(a, b, sem.at[n]) for n, (a, b) in enumerate(copies)]
+    for cp in copies:
+        cp.start()
+    for cp in copies:
+        cp.wait()
+
+
+def hand_over(*arrays):
+    anywhere = pl.BlockSpec(memory_space=pl.ANY)
+    return pl.pallas_call(
+        hand_over_kernel,
+        out_shape=tuple(jax.ShapeDtypeStruct(a.shape, a.dtype) for a in arrays),
+        in_specs=[anywhere] * 5,
+        out_specs=(anywhere,) * 5,
+        scratch_shapes=[pltpu.SemaphoreType.DMA((15,))],
+        compiler_params=pltpu.CompilerParams(vmem_limit_bytes=62 << 20),
+        name="hand_over",
+    )(*arrays)
+
+
 def per_device(
     sequence_stack,
     feature_multiplier,
@@ -664,6 +692,7 @@
         emitted_map,
         emitted_offset.reshape(1, 128),
     )
+    pu, adj, fac, bias, w = hand_over(pu, adj, fac, bias, w)
     return (
         pu.reshape(32, 128, 128),
         adj,

time: 71.4 us -> 179 us (2.51)
  Pallas kernels: 64.9 us -> 178 us
  local copies, waits for them, and re-layouts: 5.73 us -> 0 us
    pallas_call x0 -> x1, Pallas kernels: none -> 114 us  [hand_over(): pl.pallas_call(hand_over_kernel, out_shape=tuple((jax.ShapeDtypeStruct(a....]
    unnamed x13 -> x0, local copies, waits for them, and re-layouts: 5.73 us -> none
where the time goes in v6:
time: 179 us; the launch traced here: 178 us
  Pallas kernels  178 us (99%)
    pallas_call x1, Pallas kernels, hand_over(): pl.pallas_call(hand_over_kernel, out_shape=tuple((jax.ShapeDtypeStruct(a....  114 us
    pallas_call x1, Pallas kernels, run(): pl.pallas_call(kernel, out_shape=(jax.ShapeDtypeStruct((4096, 128), BF16)...  63.4 us

profile of v6, /device:TPU:1, one launch (start us, length us, event | category | flops | bytes accessed | tf_op | source)
XLA Modules:
  0.0 178.4 jit_solution(4902275507205051640)
XLA Ops:
  0.6 63.4 %outer_product_mean.1 = (bf16[4096,128]{1,0:T(8,128)(2,1)}, f32[64,32,256]{2,1,0:T(8,128)}, f32[2,32,256]{2,1,0:T(8,128)}, f32[1,128]{1,0:T(1,128)}, f32[32,32,128]{2,1,0:T(8,128)}) custom-call(bf16[64,32,256]{2,1,0:T(8,128)(2,1)} %x_ref.1, f32[1,256]{1,0:T(1,128)} %bitcast.12, bf16[32,256]{1,0:T(8,128)(2,1)} %bitcast.10, bf16[32,256]{1,0:T(8,128)(2,1)} %bitcast.11, ...), custom_call_target="tpu_custom_call" | custom-call | tf_op jit(solution)/shard_map/outer_product_mean/pallas_call | solution.py:614
  64.0 114.4 %hand_over.1 = (bf16[4096,128]{1,0:T(8,128)(2,1)}, f32[64,32,256]{2,1,0:T(8,128)}, f32[2,32,256]{2,1,0:T(8,128)}, f32[1,128]{1,0:T(1,128)}, f32[32,32,128]{2,1,0:T(8,128)}) custom-call(bf16[4096,128]{1,0:T(8,128)(2,1)} %get-tuple-element.15.refs_0_, f32[64,32,256]{2,1,0:T(8,128)} %get-tuple-element.16.refs_1_, f32[2,32,256]{2,1,0:T(8,128)} %get-tuple-element.17.refs_2_, ...), custom_call_target="tpu_custom_call" | custom-call | tf_op jit(solution)/shard_map/hand_over/pallas_call | solution.py:666

commit v7 on v6

--- a/solution.py
+++ b/solution.py
@@ -666,7 +666,7 @@
     return pl.pallas_call(
         hand_over_kernel,
         out_shape=tuple(jax.ShapeDtypeStruct(a.shape, a.dtype) for a in arrays),
-        in_specs=[anywhere] * 5,
+        in_specs=[pl.BlockSpec(memory_space=pltpu.VMEM)] * 5,
         out_specs=(anywhere,) * 5,
         scratch_shapes=[pltpu.SemaphoreType.DMA((15,))],
         compiler_params=pltpu.CompilerParams(vmem_limit_bytes=62 << 20),

time: 179 us -> 68.1 us (0.38)
  Pallas kernels: 178 us -> 67.4 us
    pallas_call x1, Pallas kernels: 114 us -> 4 us  [hand_over(): pl.pallas_call(hand_over_kernel, out_shape=tuple((jax.ShapeDtypeStruct(a....]
where the time goes in v7:
time: 68.1 us; the launch traced here: 68 us
  Pallas kernels  67.4 us (99%)
    pallas_call x1, Pallas kernels, run(): pl.pallas_call(kernel, out_shape=(jax.ShapeDtypeStruct((4096, 128), BF16)...  63.4 us
    pallas_call x1, Pallas kernels, hand_over(): pl.pallas_call(hand_over_kernel, out_shape=tuple((jax.ShapeDtypeStruct(a....  4 us

profile of v7, /device:TPU:1, one launch (start us, length us, event | category | flops | bytes accessed | tf_op | source)
XLA Modules:
  0.0 68.0 jit_solution(4276627731574280652)
XLA Ops:
  0.6 63.4 %outer_product_mean.1 = (bf16[4096,128]{1,0:T(8,128)(2,1)}, f32[64,32,256]{2,1,0:T(8,128)}, f32[2,32,256]{2,1,0:T(8,128)}, f32[1,128]{1,0:T(1,128)}, f32[32,32,128]{2,1,0:T(8,128)}) custom-call(bf16[64,32,256]{2,1,0:T(8,128)(2,1)} %x_ref.1, f32[1,256]{1,0:T(1,128)} %bitcast.12, bf16[32,256]{1,0:T(8,128)(2,1)} %bitcast.10, bf16[32,256]{1,0:T(8,128)(2,1)} %bitcast.11, ...), custom_call_target="tpu_custom_call" | custom-call | tf_op jit(solution)/shard_map/outer_product_mean/pallas_call | solution.py:614
  64.0 4.0 %hand_over.1 = (bf16[4096,128]{1,0:T(8,128)(2,1)}, f32[64,32,256]{2,1,0:T(8,128)}, f32[2,32,256]{2,1,0:T(8,128)}, f32[1,128]{1,0:T(1,128)}, f32[32,32,128]{2,1,0:T(8,128)}) custom-call(bf16[4096,128]{1,0:T(8,128)(2,1)} %get-tuple-element.15.refs_0_, f32[64,32,256]{2,1,0:T(8,128)} %get-tuple-element.16.refs_1_, f32[2,32,256]{2,1,0:T(8,128)} %get-tuple-element.17.refs_2_, ...), custom_call_target="tpu_custom_call" | custom-call | tf_op jit(solution)/shard_map/hand_over/pallas_call | solution.py:666
